TPU v7x, 32 devices: a whole 2x2x4 slice. The times are simulated.
32 devices in a mesh: dp: 2 (over x), ctx: 16 (over z, y, core).
Axes of the slice: x: 2, y: 2, z: 4, core: 2. Of those that a mesh axis runs over, the one named last changes fastest.
Arguments:
- fwd_proj: bfloat16 [4096, 3072], P(('dp', 'ctx')), parts along dimension 0, may hold values from -6 to 6
- rev_proj: bfloat16 [4096, 3072], P(('dp', 'ctx')), parts along dimension 0, may hold values from -6 to 6
- tokens: int32 [4096], P(('dp', 'ctx')), parts along dimension 0, may hold values from 0 to 4
- short_taps: float32 [3, 3072], replicated, may hold values from -3.5 to 3.5
- long_kernel: float32 [1024, 2048], P('ctx'), may hold values from -1 to 1
- skip_gain: float32 [1024], P('ctx'), may hold values from -4 to 4
- out_weight: bfloat16 [1024, 1024], replicated, may hold values from -0.1875 to 0.1875
Outputs:
- mixed: bfloat16 [4096, 1024], P(('dp', 'ctx')), parts along dimension 0
There are 2 independent parts, one for each index of `dp`. A program takes and returns all parts, laid end to end along the dimension named above; an argument that names none is the same for every part. Nothing has to cross between parts.
Inputs may be any that keep to these rules, and one draw needn't show every extreme that they name: `tokens`: base of each position, 0 to 3 for A, C, G, T and 4 for an unknown base N.
All inputs are finite; a program needn't handle non-finite values.
Results may differ from a plain program's by a relative error of at most 0.0064.
Values may be sent and summed in bfloat16 or wider, within the bound.
No kernel may reach another device: no remote copies, remote signals or barrier semaphores. Data moves between devices by JAX's collectives and lax.ppermute only.
A program may use at most 64 MiB of HBM per device.

v0:
```python
import math

import jax
import jax.numpy as jnp
from jax import lax
from jax.sharding import PartitionSpec as P


def shifted(value, axis, steps):
    count = lax.axis_size(axis)
    leading, last = (max(0, -steps), min(count, count - steps))
    return lax.ppermute(value, axis, [(source, source + steps) for source in range(leading, last)])


def angle_table(rows, cols, period):
    row_index = lax.broadcasted_iota(jnp.int32, (rows, cols), 0)
    col_index = lax.broadcasted_iota(jnp.int32, (rows, cols), 1)
    phase = (row_index * col_index % period).astype(jnp.float32) * (2.0 * math.pi / period)
    return (jnp.cos(phase), -jnp.sin(phase))


def left_product(matrix, signal):
    return jnp.einsum("kn,cnm->ckm", matrix, signal, precision=lax.Precision.HIGHEST)


def right_product(signal, matrix):
    return jnp.einsum("ckn,nm->ckm", signal, matrix, precision=lax.Precision.HIGHEST)


def make_tables(length):
    half = length // 128
    outer = 2 * half
    return (
        angle_table(outer, outer, outer),
        angle_table(outer, 128, outer * 128),
        angle_table(128, 128, 128),
    )


def forward_spectrum(real_part, imag_part, tables):
    (outer_cos, outer_sin), (twist_cos, twist_sin), (inner_cos, inner_sin) = tables
    half = real_part.shape[1]
    left_cos = outer_cos[:, :half]
    left_sin = outer_sin[:, :half]
    if imag_part is None:
        section_real = left_product(left_cos, real_part)
        section_imag = left_product(left_sin, real_part)
    else:
        section_real = left_product(left_cos, real_part) - left_product(left_sin, imag_part)
        section_imag = left_product(left_cos, imag_part) + left_product(left_sin, real_part)
    turned_real = section_real * twist_cos - section_imag * twist_sin
    turned_imag = section_real * twist_sin + section_imag * twist_cos
    spec_real = right_product(turned_real, inner_cos) - right_product(turned_imag, inner_sin)
    spec_imag = right_product(turned_real, inner_sin) + right_product(turned_imag, inner_cos)
    return (spec_real, spec_imag)


def inverse_signal(spec_real, spec_imag, tables):
    (outer_cos, outer_sin), (twist_cos, twist_sin), (inner_cos, inner_sin) = tables
    half = outer_cos.shape[0] // 2
    total = float(outer_cos.shape[0] * 128)
    section_real = right_product(spec_real, inner_cos) + right_product(spec_imag, inner_sin)
    section_imag = right_product(spec_imag, inner_cos) - right_product(spec_real, inner_sin)
    turned_real = section_real * twist_cos + section_imag * twist_sin
    turned_imag = section_imag * twist_cos - section_real * twist_sin
    row_cos = outer_cos[:half]
    row_sin = outer_sin[:half]
    out_real = (left_product(row_cos, turned_real) + left_product(row_sin, turned_imag)) / total
    out_imag = (left_product(row_cos, turned_imag) - left_product(row_sin, turned_real)) / total
    return (out_real, out_imag)


def times_kernel(spec_real, spec_imag, kernel_real, kernel_imag):
    return (
        spec_real * kernel_real - spec_imag * kernel_imag,
        spec_real * kernel_imag + spec_imag * kernel_real,
    )


def per_device(fwd_proj, rev_proj, tokens, short_taps, long_kernel, skip_gain, out_weight):
    width = fwd_proj.shape[1] // 3
    low_rows = shifted(fwd_proj[-2:], "ctx", 1)
    high_rows = shifted(rev_proj[:2], "ctx", -1)
    fwd_ext = jnp.concatenate([low_rows, fwd_proj], axis=0).astype(jnp.float32)
    rev_ext = jnp.concatenate([rev_proj, high_rows], axis=0).astype(jnp.float32)
    fwd_mixed = (
        short_taps[0] * fwd_ext[2:] + short_taps[1] * fwd_ext[1:-1] + short_taps[2] * fwd_ext[:-2]
    )
    rev_mixed = (
        short_taps[0] * rev_ext[:-2] + short_taps[1] * rev_ext[1:-1] + short_taps[2] * rev_ext[2:]
    )
    known = (tokens != 4).astype(jnp.float32)[:, None]
    fwd_input = (known * fwd_mixed[:, width : 2 * width] * fwd_mixed[:, :width]).astype(
        jnp.bfloat16
    )
    rev_input = (known * rev_mixed[:, width : 2 * width] * rev_mixed[:, :width]).astype(
        jnp.bfloat16
    )
    count, length = long_kernel.shape
    tables = make_tables(length)
    kernel_spec = forward_spectrum(long_kernel.reshape(count, length // 128, 128), None, tables)
    paired = jnp.stack([fwd_input.T, rev_input.T], axis=1)
    pair_channels = lax.all_to_all(paired, "ctx", split_axis=0, concat_axis=2, tiled=True)
    fwd_signal = pair_channels[:, 0].astype(jnp.float32)
    rev_signal = jnp.flip(pair_channels[:, 1], 1).astype(jnp.float32)
    spec_real, spec_imag = forward_spectrum(
        fwd_signal.reshape(count, length // 128, 128),
        rev_signal.reshape(count, length // 128, 128),
        tables,
    )
    prod_real, prod_imag = times_kernel(spec_real, spec_imag, kernel_spec[0], kernel_spec[1])
    out_real, out_imag = inverse_signal(prod_real, prod_imag, tables)
    fwd_out = (out_real.reshape(count, length) + skip_gain[:, None] * fwd_signal).astype(
        jnp.bfloat16
    )
    rev_flipped = out_imag.reshape(count, length) + skip_gain[:, None] * rev_signal
    rev_out = jnp.flip(rev_flipped, 1).astype(jnp.bfloat16)
    stacked = jnp.stack([fwd_out, rev_out], axis=1)
    returned = lax.all_to_all(stacked, "ctx", split_axis=2, concat_axis=0, tiled=True)
    fwd_rows = returned[:, 0, :].T.astype(jnp.float32)
    rev_rows = returned[:, 1, :].T.astype(jnp.float32)
    fwd_gated = fwd_mixed[:, 2 * width :] * fwd_rows
    rev_gated = rev_mixed[:, 2 * width :] * rev_rows
    combined = (fwd_gated + jnp.flip(rev_gated, 1)).astype(jnp.bfloat16)
    return jnp.dot(combined, out_weight, preferred_element_type=jnp.float32).astype(jnp.bfloat16)


def solution(mesh):
    in_specs = (
        P(("dp", "ctx"), None),
        P(("dp", "ctx"), None),
        P(("dp", "ctx")),
        P(),
        P("ctx", None),
        P("ctx"),
        P(),
    )
    out_specs = P(("dp", "ctx"), None)
    return jax.shard_map(
        per_device, mesh=mesh, in_specs=in_specs, out_specs=out_specs, check_vma=False
    )
```

profile of v0, /device:TPU:0, one launch (start us, length us, event | category | flops | bytes accessed | tf_op | source)
XLA Modules:
  0.0 122.6 jit_solution(13808383429421346804)
XLA Ops:
  0.0 1.0 slice.93
  1.0 2.4 %collective-permute-start = (bf16[2,3072]{1,0:T(2,128)(2,1)S(1)}, bf16[2,3072]{1,0:T(2,128)(2,1)S(1)}, u32[]{:S(2)}, u32[]{:S(2)}) collective-permute-start(bf16[2,3072]{1,0:T(2,128)(2,1)S(1)} %slice.93), channel_id=1, source_target_pairs={{0,1},{1,2},{2,3},{3,4},{4,5},{5,6},{6,7},{7,8},{8,9},{9,10},{10,1... | collective-permute-start | bytes 36872 | tf_op jit(solution)/shard_map/ppermute | solution.py:12
  3.3 0.8 slice.102
  4.1 1.3 %collective-permute-start.1 = (bf16[2,3072]{1,0:T(2,128)(2,1)S(1)}, bf16[2,3072]{1,0:T(2,128)(2,1)S(1)}, u32[]{:S(2)}, u32[]{:S(2)}) collective-permute-start(bf16[2,3072]{1,0:T(2,128)(2,1)S(1)} %slice.102), channel_id=1, source_target_pairs={{1,0},{2,1},{3,2},{4,3},{5,4},{6,5},{7,6},{8,7},{9,8},{10,9},{11,1... | collective-permute-start | bytes 36872 | tf_op jit(solution)/shard_map/ppermute | solution.py:12
  5.6 0.9 fusion.119
  6.6 1.1 copy.59
  7.7 1.0 fusion.70
  8.8 2.0 %fusion.67 = f32[32,64,128]{2,0,1:T(8,128)} fusion(f32[64,16,128]{2,1,0:T(8,128)S(1)} %bitcast.139, f32[32,32]{0,1:T(8,128)S(1)} %fusion.66), kind=kOutput, calls=%fused_computation.121 | convolution fusion | flops 50331648 | bytes 1581056 | tf_op jit(solution)/shard_map/kn,cnm->ckm/dot_general | solution.py:23
  10.8 2.3 %copy.33 = bf16[128,3072]{0,1:T(8,128)(2,1)} copy(bf16[128,3072]{1,0:T(8,128)(2,1)} %param.7) | data formatting | bytes 1572864 | tf_op args[0]
  13.2 2.3 %copy.34 = bf16[128,3072]{0,1:T(8,128)(2,1)} copy(bf16[128,3072]{1,0:T(8,128)(2,1)} %param.8) | data formatting | bytes 1572864 | tf_op args[1]
  15.5 1.2 %copy.32 = bf16[2,3072]{0,1:T(8,128)(2,1)} copy(bf16[2,3072]{1,0:T(2,128)(2,1)S(1)} %collective-permute-done) | data formatting | bytes 24576 | tf_op jit(solution)/shard_map/ppermute | solution.py:12
  16.7 3.6 %maximum_convert_fusion = f32[130,3072]{0,1:T(8,128)} fusion(bf16[128,3072]{0,1:T(8,128)(2,1)} %copy.33, bf16[2,3072]{0,1:T(8,128)(2,1)} %copy.32), kind=kLoop, calls=%fused_computation.10 | loop fusion | flops 1597440 | bytes 2396160 | tf_op jit(solution)/shard_map/convert_element_type | solution.py:84
  20.3 1.3 %copy.35 = bf16[2,3072]{0,1:T(8,128)(2,1)} copy(bf16[2,3072]{1,0:T(2,128)(2,1)S(1)} %collective-permute-done.1) | data formatting | bytes 24576 | tf_op jit(solution)/shard_map/ppermute | solution.py:12
  21.6 1.8 %maximum_convert_fusion.1 = f32[130,3072]{0,1:T(8,128)S(1)} fusion(bf16[2,3072]{0,1:T(8,128)(2,1)} %copy.35, bf16[128,3072]{0,1:T(8,128)(2,1)} %copy.34), kind=kLoop, calls=%fused_computation.11 | loop fusion | flops 1597440 | bytes 2396160 | tf_op jit(solution)/shard_map/convert_element_type | solution.py:85
  24.0 3.2 %fusion.2 = (f32[128,3072]{0,1:T(8,128)S(1)}, f32[128,3072]{0,1:T(8,128)S(1)}) fusion(f32[130,3072]{0,1:T(8,128)S(1)} %copy-done.3, f32[3072]{0:T(1024)S(1)} %bitcast.156, f32[3072]{0:T(1024)S(1)} %bitcast.157, f32[3072]{0:T(1024)S(1)} %bitcast.155, f32[130,3072]{0,1:T(8,128)S(1)} %maximum_convert_fusion.1), kind=kLoop, calls=%fused_computation.6 | loop fusion | flops 3932160 | bytes 12619776 | tf_op jit(solution)/shard_map/add | solution.py:87
  27.3 1.0 copy-done.4
  28.8 1.3 %copy.36 = bf16[1024,2,128]{2,1,0:T(2,128)(2,1)} copy(bf16[1024,2,128]{2,0,1:T(8,128)(2,1)S(1)} %pad_maximum_fusion) | data formatting | bytes 1048576 | tf_op jit(solution)/shard_map/stack | solution.py:102
  30.1 9.3 %all-to-all-start = ((bf16[1024,2,128]{2,1,0:T(2,128)(2,1)}), bf16[1024,2,128]{2,1,0:T(2,128)(2,1)}, u32[]{:S(2)}, u32[]{:S(2)}) async-start(bf16[1024,2,128]{2,1,0:T(2,128)(2,1)} %copy.36), calls=%async_computation | async-start | bytes 1048576 | tf_op jit(solution)/shard_map/all_to_all | solution.py:103
  39.5 2.5 %fusion.13 = f32[64,32,128]{2,1,0:T(8,128)S(1)} fusion(f32[32,64,128]{2,0,1:T(8,128)S(1)} %fusion.70, f32[32,64,128]{2,0,1:T(8,128)} %fusion.67, f32[32,128]{1,0:T(8,128)S(1)} %get-tuple-element.16, f32[32,128]{1,0:T(8,128)S(1)} %get-tuple-element.17), kind=kOutput, calls=%fused_computation.32 | convolution fusion | flops 403668992 | bytes 3178496 | tf_op jit(solution)/shard_map/ckn,nm->ckm/dot_general | solution.py:27
  42.0 1.2 %fusion.11 = f32[64,32,128]{2,1,0:T(8,128)S(1)} fusion(f32[32,64,128]{2,0,1:T(8,128)S(1)} %fusion.70, f32[32,64,128]{2,0,1:T(8,128)S(1)} %copy-done.1, f32[32,128]{1,0:T(8,128)S(1)} %get-tuple-element.16, f32[32,128]{1,0:T(8,128)S(1)} %get-tuple-element.17), kind=kOutput, calls=%fused_computation.30 | convolution fusion | flops 403685376 | bytes 3178496 | tf_op jit(solution)/shard_map/ckn,nm->ckm/dot_general | solution.py:27
  43.3 2.2 %convolution_subtract_fusion.1 = f32[64,32,128]{2,1,0:T(8,128)} fusion(f32[64,32,128]{2,1,0:T(8,128)S(1)} %fusion.13, f32[32,64,128]{2,0,1:T(8,128)S(1)} %fusion.70, f32[32,64,128]{2,0,1:T(8,128)S(1)} %copy-done.1, f32[32,128]{1,0:T(8,128)S(1)} %get-tuple-element.16, f32[32,128]{1,0:T(8,128)S(1)} %get-tuple-element.17), kind=kOutput, calls=%fused_computation.16 | convolution fusion | flops 403947520 | bytes 4227072 | tf_op jit(solution)/shard_map/ckn,nm->ckm/dot_general | solution.py:27
  45.5 2.2 %convolution_add_fusion.1 = f32[64,32,128]{2,1,0:T(8,128)} fusion(f32[64,32,128]{2,1,0:T(8,128)S(1)} %fusion.11, f32[32,64,128]{2,0,1:T(8,128)S(1)} %fusion.70, f32[32,64,128]{2,0,1:T(8,128)S(1)} %copy-done.1, f32[32,128]{1,0:T(8,128)S(1)} %get-tuple-element.16, f32[32,128]{1,0:T(8,128)S(1)} %get-tuple-element.17), kind=kOutput, calls=%fused_computation.14 | convolution fusion | flops 403931136 | bytes 4227072 | tf_op jit(solution)/shard_map/ckn,nm->ckm/dot_general | solution.py:27
  47.7 6.3 %all-to-all-done = bf16[1024,2,128]{2,1,0:T(2,128)(2,1)} async-done(((bf16[1024,2,128]{2,1,0:T(2,128)(2,1)}), bf16[1024,2,128]{2,1,0:T(2,128)(2,1)}, u32[]{:S(2)}, u32[]{:S(2)}) %all-to-all-start) | async-done | bytes 524320 | tf_op jit(solution)/shard_map/all_to_all | solution.py:103
  54.0 1.1 copy.37
  56.1 1.5 %rev.12 = bf16[64,2048]{1,0:T(8,128)(2,1)S(1)} reverse(bf16[64,2048]{1,0:T(8,128)(2,1)S(1)} %get-tuple-element.8), dimensions={1} | reverse | bytes 524288 | tf_op jit(solution)/shard_map/jit(_flip)/rev | solution.py:105
  60.2 1.2 %fusion.20 = f32[64,32,128]{2,1,0:T(8,128)S(1)} fusion(f32[64,32,128]{2,1,0:T(8,128)S(1)} %fusion.4, f32[64,32,128]{2,1,0:T(8,128)S(1)} %fusion.5, f32[32,128]{1,0:T(8,128)S(1)} %get-tuple-element.16, f32[32,128]{1,0:T(8,128)S(1)} %get-tuple-element.17), kind=kOutput, calls=%fused_computation.60 | convolution fusion | flops 403668992 | bytes 3178496 | tf_op jit(solution)/shard_map/ckn,nm->ckm/dot_general | solution.py:27
  61.5 1.2 %fusion.19 = f32[64,32,128]{2,1,0:T(8,128)S(1)} fusion(f32[64,32,128]{2,1,0:T(8,128)S(1)} %fusion.4, f32[64,32,128]{2,1,0:T(8,128)S(1)} %fusion.5, f32[32,128]{1,0:T(8,128)S(1)} %get-tuple-element.16, f32[32,128]{1,0:T(8,128)S(1)} %get-tuple-element.17), kind=kOutput, calls=%fused_computation.59 | convolution fusion | flops 403685376 | bytes 3178496 | tf_op jit(solution)/shard_map/ckn,nm->ckm/dot_general | solution.py:27
  62.7 1.3 %convolution_subtract_fusion.2 = f32[64,32,128]{2,1,0:T(8,128)S(1)} fusion(f32[64,32,128]{2,1,0:T(8,128)S(1)} %fusion.20, f32[64,32,128]{2,1,0:T(8,128)S(1)} %fusion.4, f32[64,32,128]{2,1,0:T(8,128)S(1)} %fusion.5, f32[32,128]{1,0:T(8,128)S(1)} %get-tuple-element.16, f32[32,128]{1,0:T(8,128)S(1)} %get-tuple-element.17), kind=kOutput, calls=%fused_computation.17 | convolution fusion | flops 403947520 | bytes 4227072 | tf_op jit(solution)/shard_map/ckn,nm->ckm/dot_general | solution.py:27
  64.3 1.4 %multiply_add_fusion.1 = (f32[64,32,128]{2,1,0:T(8,128)S(1)}, f32[64,32,128]{2,1,0:T(8,128)S(1)}) fusion(f32[64,32,128]{2,1,0:T(8,128)S(1)} %copy-done.6, f32[64,32,128]{2,1,0:T(8,128)S(1)} %convolution_subtract_fusion.2, f32[64,32,128]{2,1,0:T(8,128)S(1)} %copy-done.7, f32[64,32,128]{2,1,0:T(8,128)S(1)} %fusion.19, f32[64,32,128]{2,1,0:T(8,128)S(1)} %fusion.4, ...), kind=kOutput, calls=%fused_computation.36 | convolution fusion | flops 405504000 | bytes 8421376 | tf_op jit(solution)/shard_map/ckn,nm->ckm/dot_general | solution.py:27
  65.7 1.2 fusion.37
  66.9 1.2 %fusion.35 = f32[64,32,128]{2,1,0:T(8,128)S(1)} fusion(f32[64,32,128]{2,1,0:T(8,128)S(1)} %get-tuple-element.5), kind=kOutput, calls=%fused_computation.82 | convolution fusion | flops 402882560 | bytes 2097152 | tf_op jit(solution)/shard_map/ckn,nm->ckm/dot_general | solution.py:27
  68.2 1.2 %convolution_add_fusion = f32[64,32,128]{2,1,0:T(8,128)S(1)} fusion(f32[64,32,128]{2,1,0:T(8,128)S(1)} %fusion.37, f32[64,32,128]{2,1,0:T(8,128)S(1)} %get-tuple-element.5), kind=kOutput, calls=%fused_computation.13 | convolution fusion | flops 403161088 | bytes 3145728 | tf_op jit(solution)/shard_map/ckn,nm->ckm/dot_general | solution.py:27
  69.4 1.5 %convolution_subtract_fusion = f32[64,32,128]{2,1,0:T(8,128)S(1)} fusion(f32[64,32,128]{2,1,0:T(8,128)S(1)} %fusion.35, f32[64,32,128]{2,1,0:T(8,128)S(1)} %get-tuple-element.6), kind=kOutput, calls=%fused_computation.12 | convolution fusion | flops 403161088 | bytes 3145728 | tf_op jit(solution)/shard_map/ckn,nm->ckm/dot_general | solution.py:27
  71.7 1.6 %fusion.21 = f32[64,128,16]{1,2,0:T(8,128)} fusion(f32[64,32,128]{2,1,0:T(8,128)S(1)} %convolution_subtract_fusion, f32[64,32,128]{2,1,0:T(8,128)S(1)} %convolution_add_fusion, f32[32,128]{1,0:T(8,128)S(1)} %get-tuple-element.16, f32[32,128]{1,0:T(8,128)S(1)} %get-tuple-element.17, f32[32,32]{0,1:T(8,128)S(1)} %fusion.66), kind=kOutput, calls=%fused_computation.61 | convolution fusion | flops 51118080 | bytes 2658304 | tf_op jit(solution)/shard_map/kn,cnm->ckm/dot_general | solution.py:23
  74.1 0.9 bitcast_add_fusion
  75.0 6.5 %rev.13 = bf16[64,2048]{1,0:T(8,128)(2,1)S(1)} reverse(bf16[64,2048]{1,0:T(8,128)(2,1)} %bitcast_add_fusion), dimensions={1} | reverse | bytes 524288 | tf_op jit(solution)/shard_map/jit(_flip)/rev | solution.py:117
  81.5 3.0 %fusion.8 = f32[64,16,128]{2,1,0:T(8,128)} fusion(f32[64,128,16]{1,2,0:T(8,128)} %fusion.21, f32[64,32,128]{2,1,0:T(8,128)S(1)} %convolution_add_fusion, f32[64,32,128]{2,1,0:T(8,128)} %copy-done.2, f32[32,128]{1,0:T(8,128)S(1)} %get-tuple-element.16, f32[32,128]{1,0:T(8,128)S(1)} %get-tuple-element.17, f32[32,32]{0,1:T(8,128)S(1)} %sine_negate_fusion.8), kind=kOutput, calls=%fused_computation.26 | convolution fusion | flops 51380224 | bytes 3182592 | tf_op jit(solution)/shard_map/kn,cnm->ckm/dot_general | solution.py:23
  84.5 1.1 reshape.58
  85.6 1.1 add_convert_fusion
  86.7 0.8 pad_maximum_fusion.1
  87.5 2.3 %copy.43 = bf16[64,2,2048]{0,1,2:T(2,128)(2,1)S(1)} copy(bf16[64,2,2048]{2,0,1:T(8,128)(2,1)} %pad_maximum_fusion.1) | data formatting | bytes 1048576 | tf_op jit(solution)/shard_map/stack | solution.py:118
  89.9 1.5 %reshape.70 = bf16[16,2,8192]{2,1,0:T(2,128)(2,1)} reshape(bf16[2048,2,64]{2,1,0:T(2,128)(2,1)S(1)} %bitcast.140) | data formatting | bytes 1048576
  91.4 18.7 %all_to_all.36 = bf16[16,2,8192]{2,1,0:T(2,128)(2,1)} all-to-all(bf16[16,2,8192]{2,1,0:T(2,128)(2,1)} %reshape.70), channel_id=1, replica_groups=mesh['dp'=2,'ctx'=16] {'ctx'}, dimensions={0} | all-to-all | bytes 1048576 | tf_op jit(solution)/shard_map/all_to_all | solution.py:119
  110.1 3.0 %reshape.71 = bf16[2048,2,64]{2,1,0:T(2,128)(2,1)S(1)} reshape(bf16[16,2,8192]{2,1,0:T(2,128)(2,1)} %all_to_all.36) | data formatting | bytes 1048576
  113.0 1.8 %copy.55 = bf16[64,2,16,128]{3,0,2,1:T(8,128)(2,1)} copy(bf16[64,2,16,128]{0,1,3,2:T(2,128)(2,1)S(1)} %bitcast.141) | data formatting | bytes 1048576 | tf_op jit(solution)/shard_map/all_to_all | solution.py:119
  114.9 2.0 %slice_multiply_fusion.6 = f32[128,1024]{0,1:T(8,128)} fusion(f32[128,3072]{0,1:T(8,128)} %copy-done.5, bf16[1024,2,128]{2,0,1:T(8,128)(2,1)} %bitcast.149), kind=kLoop, calls=%fused_computation.44 | loop fusion | flops 262144 | bytes 1310720 | tf_op jit(solution)/shard_map/mul | solution.py:123
  116.9 3.4 %rev.14 = f32[128,1024]{0,1:T(8,128)S(1)} reverse(f32[128,1024]{0,1:T(8,128)} %slice_multiply_fusion.6), dimensions={1} | reverse | bytes 1048576 | tf_op jit(solution)/shard_map/jit(_flip)/rev | solution.py:124
  120.3 2.2 %convolution_convert_fusion = bf16[128,1024]{1,0:T(8,128)(2,1)} fusion(bf16[1024,1024]{1,0:T(8,128)(2,1)S(1)} %copy-done, f32[128,1024]{0,1:T(8,128)S(1)} %rev.14, f32[128,3072]{0,1:T(8,128)} %copy-done.4, bf16[1024,2,128]{2,0,1:T(8,128)(2,1)S(1)} %bitcast.150), kind=kOutput, calls=%fused_computation.27 | convolution fusion | flops 269090816 | bytes 3670016 | tf_op jit(solution)/shard_map/dot_general | solution.py:125
  (41 shorter events, 6.9 us)
Async XLA Ops:
  0.0 120.3 %copy-start = (bf16[1024,1024]{1,0:T(8,128)(2,1)S(1)}, bf16[1024,1024]{1,0:T(8,128)(2,1)}, u32[]{:S(2)}) copy-start(bf16[1024,1024]{1,0:T(8,128)(2,1)} %param.13) | copy-start | bytes 6291460
  1.0 14.5 %collective-permute-start = (bf16[2,3072]{1,0:T(2,128)(2,1)S(1)}, bf16[2,3072]{1,0:T(2,128)(2,1)S(1)}, u32[]{:S(2)}, u32[]{:S(2)}) collective-permute-start(bf16[2,3072]{1,0:T(2,128)(2,1)S(1)} %slice.93), channel_id=1, source_target_pairs={{0,1},{1,2},{2,3},{3,4},{4,5},{5,6},{6,7},{7,8},{8,9},{9,10},{10,1... | collective-permute-start | bytes 36872 | tf_op jit(solution)/shard_map/ppermute | solution.py:12
  4.1 16.2 %collective-permute-start.1 = (bf16[2,3072]{1,0:T(2,128)(2,1)S(1)}, bf16[2,3072]{1,0:T(2,128)(2,1)S(1)}, u32[]{:S(2)}, u32[]{:S(2)}) collective-permute-start(bf16[2,3072]{1,0:T(2,128)(2,1)S(1)} %slice.102), channel_id=1, source_target_pairs={{1,0},{2,1},{3,2},{4,3},{5,4},{6,5},{7,6},{8,7},{9,8},{10,9},{11,1... | collective-permute-start | bytes 36872 | tf_op jit(solution)/shard_map/ppermute | solution.py:12
  7.7 3.0 %copy-start.11 = (s32[128]{0:T(128)S(1)}, s32[128]{0:T(128)}, u32[]{:S(2)}) copy-start(s32[128]{0:T(128)} %param.9) | copy-start | bytes 1540
  21.6 2.4 %copy-start.3 = (f32[130,3072]{0,1:T(8,128)S(1)}, f32[130,3072]{0,1:T(8,128)}, u32[]{:S(2)}) copy-start(f32[130,3072]{0,1:T(8,128)} %maximum_convert_fusion) | copy-start | bytes 4792324
  27.1 1.2 copy-start.4
  27.1 1.6 %copy-start.5 = (f32[128,3072]{0,1:T(8,128)}, f32[128,3072]{0,1:T(8,128)S(1)}, u32[]{:S(2)}) copy-start(f32[128,3072]{0,1:T(8,128)S(1)} %get-tuple-element.13) | copy-start | bytes 4718596
  30.1 23.9 %all-to-all-start = ((bf16[1024,2,128]{2,1,0:T(2,128)(2,1)}), bf16[1024,2,128]{2,1,0:T(2,128)(2,1)}, u32[]{:S(2)}, u32[]{:S(2)}) async-start(bf16[1024,2,128]{2,1,0:T(2,128)(2,1)} %copy.36), calls=%async_computation | async-start | bytes 1048576 | tf_op jit(solution)/shard_map/all_to_all | solution.py:103
  39.5 2.6 %copy-start.1 = (f32[32,64,128]{2,0,1:T(8,128)S(1)}, f32[32,64,128]{2,0,1:T(8,128)}, u32[]{:S(2)}) copy-start(f32[32,64,128]{2,0,1:T(8,128)} %fusion.67) | copy-start | bytes 3145732
  55.2 0.8 copy-start.8
  62.7 1.3 %copy-start.6 = (f32[64,32,128]{2,1,0:T(8,128)S(1)}, f32[64,32,128]{2,1,0:T(8,128)}, u32[]{:S(2)}) copy-start(f32[64,32,128]{2,1,0:T(8,128)} %convolution_subtract_fusion.1) | copy-start | bytes 3145732
  62.7 1.5 %copy-start.7 = (f32[64,32,128]{2,1,0:T(8,128)S(1)}, f32[64,32,128]{2,1,0:T(8,128)}, u32[]{:S(2)}) copy-start(f32[64,32,128]{2,1,0:T(8,128)} %convolution_add_fusion.1) | copy-start | bytes 3145732
  70.9 2.4 %copy-start.2 = (f32[64,32,128]{2,1,0:T(8,128)}, f32[64,32,128]{2,1,0:T(8,128)S(1)}, u32[]{:S(2)}) copy-start(f32[64,32,128]{2,1,0:T(8,128)S(1)} %convolution_subtract_fusion) | copy-start | bytes 3145732
  73.3 0.8 copy-start.10
  114.9 5.4 %copy-start.9 = (bf16[64,2,16,128]{3,0,2,1:T(8,128)(2,1)S(1)}, bf16[64,2,16,128]{3,0,2,1:T(8,128)(2,1)}, u32[]{:S(2)}) copy-start(bf16[64,2,16,128]{3,0,2,1:T(8,128)(2,1)} %copy.55) | copy-start | bytes 1572868
where the time goes:
time: 124 us; the launch traced here: 123 us
  local copies, waits for them, and re-layouts  38 us (31%)
  matrix products  32.3 us (26%)
  blocking collectives  18.7 us (15%)
  other arithmetic  13.8 us (11%)
  starting transfers between devices  13 us (10%)
  waiting for transfers between devices  6.31 us (5%)
    all_to_all x1, blocking collectives, per_device(): lax.all_to_all(stacked, 'ctx', split_axis=2, concat_axis=0, tiled=True)  18.7 us
    dot_general x12, matrix products, right_product(): jnp.einsum('ckn,nm->ckm', signal, matrix, precision=lax.Precision.HIGHEST)  18.5 us
    unnamed x32, local copies, waits for them, and re-layouts  13.5 us
    dot_general x10, matrix products, left_product(): jnp.einsum('kn,cnm->ckm', matrix, signal, precision=lax.Precision.HIGHEST)  11.6 us
    all_to_all x1, starting transfers between devices, per_device(): lax.all_to_all(paired, 'ctx', split_axis=0, concat_axis=2, tiled=True)  9.34 us
    rev x1, local copies, waits for them, and re-layouts, per_device(): rev_out = jnp.flip(rev_flipped, 1).astype(jnp.bfloat16)  6.47 us
    all_to_all x1, waiting for transfers between devices, per_device(): lax.all_to_all(paired, 'ctx', split_axis=0, concat_axis=2, tiled=True)  6.3 us
    ppermute x2, starting transfers between devices, shifted(): lax.ppermute(value, axis, [(source, source + steps) for source in range(l...  3.65 us
  transfers between devices with their start and end apart: 3, of which 1 were waited for; matrix products, arithmetic and copies ran while one was open for 19% of the time, Pallas kernels for 0%

commit v1 on v0

v1 whole, which is shorter than its diff:
```python
import functools

import jax
import jax.numpy as jnp
import ml_dtypes
import numpy as np
from jax import lax
from jax.experimental import pallas as pl
from jax.experimental.pallas import tpu as pltpu
from jax.sharding import PartitionSpec as P

OUTER = 32
HALF = OUTER // 2
BINS = HALF + 1
PAIRS = (BINS + 1) // 2
EXTRA = 8
LANES = 128
TILE = 16
CHUNK = 32
BIN_GROUP = 6
VMEM_BYTES = 30 * 1024 * 1024
EDGE_LANES = 256
EDGE_ROWS = 2
FULL_VMEM_BYTES = 60000000


def split_table(table):
    high = table.astype(np.float32).astype(ml_dtypes.bfloat16)
    low = (table - high.astype(np.float64)).astype(np.float32).astype(ml_dtypes.bfloat16)
    return np.stack([high, low])


def outer_rows():
    rows = [(0, 0), (HALF, 0)]
    for bin_index in range(1, HALF):
        rows += [(bin_index, 0), (bin_index, 1)]
    return rows


def dft_tables(length):
    inner = length // HALF
    total = 2 * length
    blocks = np.arange(HALF)
    enter = np.zeros((OUTER, HALF))
    for row, (bin_index, part) in enumerate(outer_rows()):
        phase = 2.0 * np.pi * (bin_index * blocks % OUTER) / OUTER
        enter[row] = -np.sin(phase) if part else np.cos(phase)
    angles = 2.0 * np.pi * (np.outer(np.arange(inner), np.arange(inner)) % inner) / inner
    cos, sin = np.cos(angles), np.sin(angles)
    mix = np.block([[cos, sin], [-sin, cos]])
    turn = np.zeros((inner, LANES))
    turn_phase = 2.0 * np.pi * np.outer(np.arange(inner), np.arange(BINS)) / total
    turn[:, :BINS] = np.cos(turn_phase)
    turn[:, LANES // 2 : LANES // 2 + BINS] = np.sin(turn_phase)
    core = np.repeat(split_table(enter).astype(np.float32), TILE, axis=2)
    return (
        core,
        split_table(mix),
        turn.astype(np.float32),
    )


def dot(left, right):
    return jnp.dot(left, right, preferred_element_type=jnp.float32)


def table_dot(table_ref, right):
    return dot(table_ref[0], right) + dot(table_ref[1], right)


def lanes_of(shape):
    return lax.broadcasted_iota(jnp.int32, shape, len(shape) - 1)


def swap(value):
    lanes = value.shape[1]
    if lanes == LANES:
        return pltpu.roll(value, lanes // 2, 1)
    return jnp.concatenate([value[:, lanes // 2 :], value[:, : lanes // 2]], axis=1)


def left_halves(one, two):
    value = one if one is not None else two
    left = lanes_of(value.shape) < value.shape[1] // 2
    one = jnp.zeros_like(value) if one is None else one
    two = jnp.zeros_like(value) if two is None else swap(two)
    return jnp.where(left, one, two)


def right_halves(one, two):
    value = one if one is not None else two
    left = lanes_of(value.shape) < value.shape[1] // 2
    one = jnp.zeros_like(value) if one is None else swap(one)
    two = jnp.zeros_like(value) if two is None else two
    return jnp.where(left, one, two)


def slot(bin_index, part):
    if bin_index >= BINS or (part and bin_index in (0, HALF)):
        return None
    if bin_index in (0, HALF):
        return bin_index // HALF
    return 2 * bin_index + part


def enter_stage(load, dots, turn_ref, per, half_rows, put):
    inner = 2 * per * half_rows
    for group in range(per):
        for tile in range(0, half_rows // TILE, 2):
            pair = [load(group, tile), load(group, tile + 1)]
            lanes = pair[0].shape[1]
            section = dots(jnp.concatenate(pair, axis=1))
            for which in range(2):
                by_row = section[:, which * lanes : (which + 1) * lanes].reshape(OUTER, TILE, lanes)

                def part_of(bin_index, part):
                    row = slot(bin_index, part)
                    return None if row is None else by_row[row]

                for index in range(PAIRS):
                    bins = (2 * index, 2 * index + 1)
                    reals = [part_of(b, 0) for b in bins]
                    imags = [part_of(b, 1) for b in bins]
                    for side, halves in enumerate((left_halves, right_halves)):
                        start = (2 * group + side) * half_rows + (tile + which) * TILE
                        cos = turn_ref[index, 0, start : start + TILE, :]
                        sin = turn_ref[index, 1, start : start + TILE, :]
                        real = halves(*reals)
                        if imags[0] is None and imags[1] is None:
                            put(index, start, real * cos)
                            put(index, inner + start, real * -sin)
                        else:
                            imag = halves(*imags)
                            put(index, start, real * cos + imag * sin)
                            put(index, inner + start, imag * cos - real * sin)


def expand(core, target):
    row = lax.broadcasted_iota(jnp.int32, (TILE, core.shape[1]), 0)
    same = row == lanes_of(row.shape) % TILE
    for index in range(OUTER):
        wide = jnp.broadcast_to(core[index : index + 1], row.shape)
        target[index * TILE : (index + 1) * TILE, :] = jnp.where(same, wide, 0.0).astype(jnp.bfloat16)


def turn_pair(turn_ref, start, count, bin_index, lanes):
    rows = pl.ds(start, count)
    cos = jnp.broadcast_to(turn_ref[rows, bin_index : bin_index + 1], (count, lanes))
    at = LANES // 2 + bin_index
    sin = jnp.broadcast_to(turn_ref[rows, at : at + 1], (count, lanes))
    return cos, sin


def store_sections(section, turn_ref, tile, lanes, put):
    start = tile * TILE
    by_row = section.reshape(OUTER, TILE, lanes)
    for bin_index in range(BINS):
        cos, sin = turn_pair(turn_ref, start, TILE, bin_index, lanes)
        if bin_index in (0, HALF):
            real = by_row[0 if bin_index == 0 else 1]
            put(bin_index, start, real * cos, real * -sin)
        else:
            real = by_row[2 * bin_index]
            imag = by_row[2 * bin_index + 1]
            put(bin_index, start, real * cos + imag * sin, imag * cos - real * sin)


def short_filter(value, taps, later, near=None):
    rows = value.shape[0]
    row = lax.broadcasted_iota(jnp.int32, (EXTRA, LANES), 0)
    shifted = []
    for lag in (1, 2):
        moved = pltpu.roll(value, rows - lag if later else lag, 0)
        shift = EXTRA - lag if later else lag
        fill = 0.0 if near is None else pltpu.roll(near, shift, 0)
        if later:
            tail = jnp.where(row < EXTRA - lag, moved[rows - EXTRA :], fill)
            moved = jnp.concatenate([moved[: rows - EXTRA], tail], axis=0)
        else:
            head = jnp.where(row >= lag, moved[:EXTRA], fill)
            moved = jnp.concatenate([head, moved[EXTRA:]], axis=0)
        shifted.append(moved)
    return taps[0:1] * value + taps[1:2] * shifted[0] + taps[2:3] * shifted[1]


def chunk_filter(ref, start, columns, taps, later):
    end = start + CHUNK
    value = ref[start:end, columns].astype(jnp.float32)
    near = None
    if later and end < ref.shape[0]:
        near = ref[end : end + TILE, columns].astype(jnp.float32)[:EXTRA]
    elif not later and start > 0:
        near = ref[start - TILE : start, columns].astype(jnp.float32)[EXTRA:]
    return short_filter(value, taps, later, near)


def gate_kernel(
    fwd_hbm, rev_hbm, tokens_hbm, taps_hbm, out_hbm, fwd_o_hbm, rev_o_hbm,
    fwd_ref, rev_ref, fwd_edge_ref, rev_edge_ref, tokens_ref, taps_ref, out_ref, fwd_o_ref, rev_o_ref,
    first_q_ref, sems, small_sems, out_sems
):
    rows = fwd_ref.shape[0]
    width = fwd_ref.shape[1] // 2
    lanes = out_ref.shape[2]
    count = lanes // 2
    small = [
        pltpu.make_async_copy(taps_hbm, taps_ref, small_sems.at[0]),
        pltpu.make_async_copy(tokens_hbm, tokens_ref, small_sems.at[1]),
        pltpu.make_async_copy(
            fwd_hbm.at[pl.ds(rows - TILE, TILE), pl.ds(2 * width, width)],
            fwd_edge_ref,
            small_sems.at[2],
        ),
        pltpu.make_async_copy(
            rev_hbm.at[pl.ds(0, TILE), pl.ds(2 * width, width)], rev_edge_ref, small_sems.at[3]
        ),
    ]
    loads, stores = [], []
    for step in range(rows // CHUNK):
        part = (pl.ds(step * CHUNK, CHUNK), pl.ds(0, 2 * width))
        copies = [
            pltpu.make_async_copy(fwd_hbm.at[part], fwd_ref.at[part], sems.at[step, 0]),
            pltpu.make_async_copy(rev_hbm.at[part], rev_ref.at[part], sems.at[step, 1]),
        ]
        for copy in copies:
            copy.start()
        loads.append(copies)
        if step == 0:
            for copy in small:
                copy.start()
    for copy in small:
        copy.wait()
    known_row = jnp.where(tokens_ref[...] != 4, 1.0, 0.0).astype(jnp.float32)
    known = jnp.transpose(jnp.broadcast_to(known_row, (LANES, rows)))
    edge_row = lax.broadcasted_iota(jnp.int32, (EXTRA, LANES), 0)

    def piece_of(left, right, piece):
        left_shift = (LANES - piece * count) % LANES
        right_shift = (LANES + count - piece * count) % LANES
        left = pltpu.roll(left, left_shift, 1) if left_shift else left
        right = pltpu.roll(right, right_shift, 1) if right_shift else right
        return jnp.where(lanes_of(left.shape) < count, left, right)[:, :lanes].astype(jnp.bfloat16)

    def rows_of(ref, columns, start):
        return ref[start : start + TILE, columns].astype(jnp.float32)

    def with_rows(edge, rows_at, value, at):
        moved = pltpu.roll(value, (rows_at - at) % EXTRA, 0)
        return jnp.where((edge_row >= rows_at) & (edge_row < rows_at + 2), moved, edge)

    pieces = LANES // count
    for copy in loads[0]:
        copy.wait()
    for step in range(rows // CHUNK):
        start = step * CHUNK
        final = start + CHUNK == rows
        if not final:
            for copy in loads[step + 1]:
                copy.wait()
        here = slice(start, start + CHUNK)
        for block in range(width // LANES):
            low = block * LANES
            at_v = slice(low, low + LANES)
            at_q = slice(width + low, width + low + LANES)
            taps_v, taps_q = taps_ref[:, at_v], taps_ref[:, at_q]
            fwd_v = chunk_filter(fwd_ref, start, at_v, taps_v, False)
            fwd_q = chunk_filter(fwd_ref, start, at_q, taps_q, False)
            fwd_body = known[here] * fwd_q * fwd_v
            rev_v = chunk_filter(rev_ref, start, at_v, taps_v, True)
            rev_q = chunk_filter(rev_ref, start, at_q, taps_q, True)
            rev_body = known[here] * rev_q * rev_v
            if start == 0:
                part = jnp.where(known[:EXTRA] > 0.0, fwd_v[:EXTRA], jnp.inf)
                head = jnp.where(edge_row < 2, part, fwd_body[:EXTRA])
                fwd_body = jnp.concatenate([head, fwd_body[EXTRA:]], axis=0)
                first_q_ref[:, at_v] = fwd_q[:EXTRA]
            if final:
                part = jnp.where(known[rows - EXTRA :] > 0.0, rev_v[CHUNK - EXTRA :], jnp.inf)
                tail = jnp.where(edge_row >= EXTRA - 2, part, rev_body[CHUNK - EXTRA :])
                rev_body = jnp.concatenate([rev_body[: CHUNK - EXTRA], tail], axis=0)
                raw_o = rows_of(fwd_edge_ref, at_v, 0)[EXTRA:]
                edge = jnp.where(edge_row < 2, first_q_ref[:, at_v], raw_o)
                edge = with_rows(edge, 2, rows_of(fwd_ref, at_v, rows - TILE)[EXTRA:], 6)
                edge = with_rows(edge, 4, rows_of(fwd_ref, at_q, rows - TILE)[EXTRA:], 6)
                fwd_body = jnp.concatenate([fwd_body, edge], axis=0)
                place = (
                    slice(low // EDGE_LANES * EDGE_ROWS, (low // EDGE_LANES + 1) * EDGE_ROWS),
                    slice(low % EDGE_LANES, low % EDGE_LANES + LANES),
                )
                fwd_o_ref[place] = pltpu.roll(raw_o, 2, 0)[:EDGE_ROWS]
                raw_o = rows_of(rev_edge_ref, at_v, 0)[:EXTRA]
                edge = jnp.where(edge_row < 2, pltpu.roll(rev_q[CHUNK - EXTRA :], 2, 0), 0.0)
                edge = with_rows(edge, 2, rows_of(rev_ref, at_v, 0)[:EXTRA], 0)
                edge = with_rows(edge, 4, rows_of(rev_ref, at_q, 0)[:EXTRA], 0)
                rev_body = jnp.concatenate([rev_body, edge], axis=0)
                rev_o_ref[place] = raw_o[:EDGE_ROWS]
            for piece in range(pieces):
                out_ref[block * pieces + piece, start : start + fwd_body.shape[0], :] = piece_of(
                    fwd_body, rev_body, piece
                )
        part = (slice(None), pl.ds(start, CHUNK + (EXTRA if final else 0)))
        copy = pltpu.make_async_copy(out_ref.at[part], out_hbm.at[part], out_sems.at[step])
        copy.start()
        stores.append(copy)
    for at, (source, target) in enumerate(((fwd_o_ref, fwd_o_hbm), (rev_o_ref, rev_o_hbm))):
        copy = pltpu.make_async_copy(source, target, small_sems.at[4 + at])
        copy.start()
        stores.append(copy)
    for copy in stores:
        copy.wait()


def sections_kernel(
    me_ref, kernel_hbm, skip_hbm, taps_hbm, core_hbm, phase_hbm,
    high, low, own_taps_ref, core_ref, phase_ref,
    kernel_ref, skip_ref, taps_ref, wide_ref, enter_ref, turn_ref, signal, sems
):
    moves = (
        (phase_hbm, phase_ref), (kernel_hbm, kernel_ref), (skip_hbm, skip_ref),
        (taps_hbm, taps_ref), (core_hbm, wide_ref), (core_hbm.at[0], core_ref),
    )
    copies = [
        pltpu.make_async_copy(source, target, sems.at[at])
        for at, (source, target) in enumerate(moves)
    ]
    for copy in copies:
        copy.start()
    count, length = kernel_ref.shape
    lanes = 2 * count
    inner = length // HALF
    half_rows = signal.shape[2]
    rows = 2 * half_rows
    per = inner // rows
    width = taps_ref.shape[1] // 3

    copies[0].wait()
    for index in range(PAIRS):
        for part in range(2):
            columns = [part * (LANES // 2) + min(2 * index + b, BINS) for b in range(2)]
            sides = [
                jnp.broadcast_to(phase_ref[:, column : column + 1], (inner, lanes))
                for column in columns
            ]
            turn_ref[index, part] = jnp.where(lanes_of((inner, lanes)) < count, *sides)

    for copy in copies[1:5]:
        copy.wait()
    me = me_ref[0]
    per_block = LANES // count
    block = me // per_block
    shift = lax.rem(LANES - (me - block * per_block) * count, LANES)
    for which in range(2):
        column = pl.multiple_of(which * width + block * LANES, LANES)
        own = pltpu.roll(taps_ref[:, pl.ds(column, LANES)], shift, 1)
        both = jnp.where(lanes_of(own.shape) < count, own, pltpu.roll(own, count, 1))[:, :lanes]
        for tap in range(3):
            own_taps_ref[3 * which + tap : 3 * which + tap + 1, :] = both[tap : tap + 1]
    own_taps_ref[6:8, :] = jnp.zeros((2, lanes), jnp.float32)

    for start in range(0, length, rows):
        piece = kernel_ref[:, start : start + rows]
        both = jnp.concatenate([piece, pltpu.roll(piece, half_rows, 1)], axis=0)
        turned = jnp.transpose(both)[:half_rows]
        if start == 0:
            gain = skip_ref[...]
            gains = jnp.concatenate([gain, jnp.zeros_like(gain)], axis=1)
            row = lax.broadcasted_iota(jnp.int32, turned.shape, 0)
            turned = turned + jnp.where(row == 0, gains, 0.0)
        signal[start // inner, start % inner // rows] = turned

    def load(group, tile):
        return signal[:, group, tile * TILE : (tile + 1) * TILE, :].reshape(HALF * TILE, lanes)

    def enter_dots(value):
        top = value.astype(jnp.bfloat16)
        rest = (value - top.astype(jnp.float32)).astype(jnp.bfloat16)
        return table_dot(enter_ref, top) + dot(enter_ref[0], rest)

    def put(index, start, value):
        top = value.astype(jnp.bfloat16)
        high[index, start : start + TILE, :] = top
        low[index, start : start + TILE, :] = (value - top.astype(jnp.float32)).astype(jnp.bfloat16)

    for part in range(2):
        expand(wide_ref[part], enter_ref.at[part])
    enter_stage(load, enter_dots, turn_ref, per, half_rows, put)
    copies[5].wait()


def spectrum_kernel(high, low, mix_hbm, *refs):
    *spec_refs, mix_out_ref, mix_ref, sems = refs
    copies = [
        pltpu.make_async_copy(mix_hbm, mix_ref, sems.at[0]),
        pltpu.make_async_copy(mix_hbm.at[0], mix_out_ref, sems.at[1]),
    ]
    for copy in copies:
        copy.start()
    for copy in copies:
        copy.wait()
    inner = high.shape[1] // 2
    lanes = high.shape[2]
    count = lanes // 2
    length = inner * HALF
    for first in range(0, PAIRS, 2):
        group = range(first, min(first + 2, PAIRS))
        top = jnp.concatenate([high[index] for index in group], axis=1)
        rest = jnp.concatenate([low[index] for index in group], axis=1)
        spec = table_dot(mix_ref, top) + dot(mix_ref[0], rest)
        for at, index in enumerate(group):
            pair = spec[:, at * lanes : (at + 1) * lanes]
            left = lanes_of((inner, lanes)) < count
            for side in range(2):
                if 2 * index + side == BINS:
                    break
                for part in range(2):
                    here = pair[part * inner : (part + 1) * inner]
                    there = swap(here)
                    value = jnp.where(left, there, here) if side else jnp.where(left, here, there)
                    if part:
                        value = jnp.where(left, value, -value)
                    weight = (1.0 if 2 * index + side in (0, HALF) else 2.0) / (2 * length)
                    value = value * weight
                    which, place = divmod(2 * index + side, BIN_GROUP)
                    spec_refs[which][place, part * inner : (part + 1) * inner, :] = value


def mended_tiles(recv_ref, own_taps_ref, group, rows):
    blocks, per, _, lanes = recv_ref.shape
    count = lanes // 2
    taps = own_taps_ref[...]
    edge = recv_ref[:, group, rows : rows + EXTRA, :].astype(jnp.float32)
    blank = jnp.zeros((1, EXTRA, lanes), jnp.float32)
    if group > 0:
        before = recv_ref[:, group - 1, rows : rows + EXTRA, :].astype(jnp.float32)
    else:
        shifted = recv_ref[: blocks - 1, per - 1, rows : rows + EXTRA, :].astype(jnp.float32)
        before = jnp.concatenate([blank, shifted], axis=0)
    if group < per - 1:
        after = recv_ref[:, group + 1, rows : rows + EXTRA, :].astype(jnp.float32)
    else:
        shifted = recv_ref[1:, 0, rows : rows + EXTRA, :].astype(jnp.float32)
        after = jnp.concatenate([shifted, blank], axis=0)
    row = lax.broadcasted_iota(jnp.int32, (EXTRA, lanes), 0)
    lane = lax.broadcasted_iota(jnp.int32, (EXTRA, lanes), 1)
    first, last = [], []
    for block in range(blocks):
        top = recv_ref[block, group, :TILE, :].astype(jnp.float32)
        part = top[:EXTRA]
        near = before[block]
        mix_v = part + taps[2:3] * pltpu.roll(near, 6, 0)
        mix_v = mix_v + jnp.where(row == 0, taps[1:2] * pltpu.roll(near, 5, 0), 0.0)
        mix_q = edge[block] + taps[5:6] * pltpu.roll(near, 4, 0)
        mix_q = mix_q + jnp.where(row == 0, taps[4:5] * pltpu.roll(near, 3, 0), 0.0)
        fixed = jnp.where(part == jnp.inf, 0.0, mix_q * mix_v)
        fixed = jnp.where((row < 2) & (lane < count), fixed, part)
        first.append(jnp.concatenate([fixed, top[EXTRA:]], axis=0).astype(jnp.bfloat16))

        end = recv_ref[block, group, rows - TILE : rows, :].astype(jnp.float32)
        part = end[EXTRA:]
        near = after[block]
        mix_v = part + taps[2:3] * pltpu.roll(near, 4, 0)
        mix_v = mix_v + jnp.where(row == 7, taps[1:2] * pltpu.roll(near, 5, 0), 0.0)
        mix_q = pltpu.roll(edge[block], 6, 0) + taps[5:6] * pltpu.roll(near, 2, 0)
        mix_q = mix_q + jnp.where(row == 7, taps[4:5] * pltpu.roll(near, 3, 0), 0.0)
        fixed = jnp.where(part == jnp.inf, 0.0, mix_q * mix_v)
        fixed = jnp.where((row >= 6) & (lane >= count), fixed, part)
        last.append(jnp.concatenate([end[:EXTRA], fixed], axis=0).astype(jnp.bfloat16))
    return jnp.stack(first), jnp.stack(last)


def filter_kernel(recv_ref, own_taps_ref, core_ref, turn_ref, *refs):
    *spec_refs, mix_ref, out_ref, sections, returned, enter_ref = refs
    expand(core_ref[...], enter_ref)
    blocks, per, padded, lanes = recv_ref.shape
    rows = padded - EXTRA
    inner = per * rows
    tiles = rows // TILE

    def put(bin_index, start, real, imag):
        sections[bin_index, start : start + TILE, :] = real.astype(jnp.bfloat16)
        sections[bin_index, inner + start : inner + start + TILE, :] = imag.astype(jnp.bfloat16)

    for group in range(per):
        first, last = mended_tiles(recv_ref, own_taps_ref, group, rows)
        loaded = [first]
        for tile in range(1, tiles - 1):
            loaded.append(recv_ref[:, group, tile * TILE : (tile + 1) * TILE, :])
        loaded.append(last)
        loaded = [value.reshape(blocks * TILE, lanes) for value in loaded]
        def section_of(tile):
            return dot(enter_ref[...], jnp.concatenate(loaded[tile : tile + 2], axis=1))

        ahead = section_of(0)
        for tile in range(0, tiles, 2):
            section = ahead
            if tile + 2 < tiles:
                ahead = section_of(tile + 2)
            at = group * tiles + tile
            store_sections(section[:, :lanes], turn_ref, at, lanes, put)
            store_sections(section[:, lanes:], turn_ref, at + 1, lanes, put)

    def bins_from(first):
        return range(first, min(first + 2, BINS))

    def spec_of(first):
        pair = [sections[b] for b in bins_from(first)]
        return dot(mix_ref[...], jnp.concatenate(pair, axis=1))

    def back_of(first, spec):
        gains = [spec_refs[b // BIN_GROUP][b % BIN_GROUP] for b in bins_from(first)]
        gain = jnp.concatenate(gains, axis=1)
        real, imag = spec[:inner], spec[inner:]
        gain_real, gain_imag = gain[:inner], gain[inner:]
        product = jnp.concatenate(
            [real * gain_real - imag * gain_imag, -real * gain_imag - imag * gain_real], axis=0
        ).astype(jnp.bfloat16)
        return dot(mix_ref[...], product)

    def store_returned(first, back):
        for at, b in enumerate(bins_from(first)):
            real = back[:inner, at * lanes : (at + 1) * lanes]
            imag = back[inner:, at * lanes : (at + 1) * lanes]
            cos, sin = turn_pair(turn_ref, 0, inner, b, lanes)
            returned[slot(b, 0)] = (real * cos + imag * sin).astype(jnp.bfloat16)
            if b not in (0, HALF):
                returned[slot(b, 1)] = (real * sin - imag * cos).astype(jnp.bfloat16)

    ahead, behind = spec_of(0), None
    for first in range(0, BINS, 2):
        spec = ahead
        if first + 2 < BINS:
            ahead = spec_of(first + 2)
        back = back_of(first, spec)
        if behind is not None:
            store_returned(first - 2, behind)
        behind = back
    store_returned(BINS - 1, behind)

    leave = jnp.transpose(enter_ref[...])
    for tile in range(0, inner // TILE, 2):
        pair = jnp.concatenate(
            [
                returned[:, at * TILE : (at + 1) * TILE, :].reshape(OUTER * TILE, lanes)
                for at in (tile, tile + 1)
            ],
            axis=1,
        )
        value = dot(leave, pair).astype(jnp.bfloat16)
        group, place = divmod(tile, tiles)
        for at in (0, 1):
            start = (place + at) * TILE
            out_ref[:, group, start : start + TILE, :] = value[
                :, at * lanes : (at + 1) * lanes
            ].reshape(blocks, TILE, lanes)


def mixing_kernel(
    ret_ref, fwd_o_ref, rev_o_ref, fwd_ref, rev_ref, taps_ref, weight_ref, out_ref, combined, total
):
    rows = fwd_ref.shape[0]
    width = weight_ref.shape[0]
    count = ret_ref.shape[2] // 2
    pieces = LANES // count
    blocks = width // LANES
    edge_row = lax.broadcasted_iota(jnp.int32, (EXTRA, LANES), 0)
    mirror = LANES - 1 - lax.broadcasted_iota(jnp.int32, (rows, LANES), 1)

    def near_edge(edges, block, target):
        low = block * LANES
        at_row = low // EDGE_LANES * EDGE_ROWS
        start = at_row // EXTRA * EXTRA
        at_lane = low % EDGE_LANES
        tile = edges[start : start + EXTRA, at_lane : at_lane + LANES]
        shift = (target - at_row + start) % EXTRA
        return pltpu.roll(tile, shift, 0) if shift else tile

    def columns(block, which):
        chunks = [
            ret_ref[block * pieces + piece].astype(jnp.float32)[
                :, which * count : (which + 1) * count
            ]
            for piece in range(pieces)
        ]
        return jnp.concatenate(chunks, axis=1)

    for block in range(blocks):
        low = 2 * width + block * LANES
        taps = taps_ref[:, low : low + LANES]
        mixed = short_filter(fwd_ref[:, low : low + LANES].astype(jnp.float32), taps, False)
        more = jnp.where(edge_row < 2, taps[2:3] * near_edge(fwd_o_ref, block, 0), 0.0)
        last = jnp.where(edge_row == 0, taps[1:2] * near_edge(fwd_o_ref, block, -1), 0.0)
        mixed = jnp.concatenate([mixed[:EXTRA] + more + last, mixed[EXTRA:]], axis=0)
        gated = mixed * columns(block, 0)

        other = blocks - 1 - block
        low = 2 * width + other * LANES
        taps = taps_ref[:, low : low + LANES]
        mixed = short_filter(rev_ref[:, low : low + LANES].astype(jnp.float32), taps, True)
        more = jnp.where(edge_row >= 6, taps[2:3] * near_edge(rev_o_ref, other, 6), 0.0)
        first = jnp.where(edge_row == 7, taps[1:2] * near_edge(rev_o_ref, other, 7), 0.0)
        tail = mixed[rows - EXTRA :] + more + first
        mixed = jnp.concatenate([mixed[: rows - EXTRA], tail], axis=0)
        turned = jnp.take_along_axis(mixed * columns(other, 1), mirror, axis=1)
        combined[:, block * LANES : (block + 1) * LANES] = (gated + turned).astype(jnp.bfloat16)
        if block % 2:
            part = slice((block - 1) * LANES, (block + 1) * LANES)
            product = dot(combined[:, part], weight_ref[part, :])
            if block == 1:
                total[...] = product
            elif block < blocks - 1:
                total[...] += product
            else:
                out_ref[...] = (total[...] + product).astype(jnp.bfloat16)


HBM = pl.BlockSpec(memory_space=pltpu.HBM)
VMEM = pl.BlockSpec(memory_space=pltpu.VMEM)
SMEM = pl.BlockSpec(memory_space=pltpu.SMEM)


def params(limit=VMEM_BYTES):
    return pltpu.CompilerParams(vmem_limit_bytes=limit)


def cost(flops, size):
    return pl.CostEstimate(flops=flops, bytes_accessed=size, transcendentals=0)


def exchange(value):
    return lax.all_to_all(value, "ctx", split_axis=0, concat_axis=0, tiled=True)


def shifted(value, steps):
    count = lax.axis_size("ctx")
    first, end = max(0, -steps), min(count, count - steps)
    return lax.ppermute(value, "ctx", [(source, source + steps) for source in range(first, end)])


def per_device(fwd_proj, rev_proj, tokens, short_taps, long_kernel, skip_gain, out_weight):
    rows = fwd_proj.shape[0]
    half_rows = rows // 2
    width = fwd_proj.shape[1] // 3
    count, length = long_kernel.shape
    devices = length // rows
    lanes = 2 * count
    inner = length // HALF
    per = devices // HALF
    padded = rows + EXTRA
    edge_block = (EDGE_ROWS * width // EDGE_LANES, EDGE_LANES)
    tables = [jnp.asarray(table) for table in dft_tables(length)]
    core, mix, phases = tables
    outer_shape = (OUTER * TILE, HALF * TILE)
    block = (devices, padded, lanes)

    sent, fwd_o, rev_o = pl.pallas_call(
        gate_kernel,
        out_shape=(
            jax.ShapeDtypeStruct(block, jnp.bfloat16),
            jax.ShapeDtypeStruct(edge_block, jnp.float32),
            jax.ShapeDtypeStruct(edge_block, jnp.float32),
        ),
        in_specs=[HBM] * 4,
        out_specs=(HBM,) * 3,
        scratch_shapes=[
            pltpu.VMEM((rows, 2 * width), jnp.bfloat16),
            pltpu.VMEM((rows, 2 * width), jnp.bfloat16),
            pltpu.VMEM((TILE, width), jnp.bfloat16),
            pltpu.VMEM((TILE, width), jnp.bfloat16),
            pltpu.VMEM((1, rows), jnp.int32),
            pltpu.VMEM(short_taps.shape, jnp.float32),
            pltpu.VMEM(block, jnp.bfloat16),
            pltpu.VMEM(edge_block, jnp.float32),
            pltpu.VMEM(edge_block, jnp.float32),
            pltpu.VMEM((EXTRA, width), jnp.float32),
            pltpu.SemaphoreType.DMA((rows // CHUNK, 2)),
            pltpu.SemaphoreType.DMA((6,)),
            pltpu.SemaphoreType.DMA((rows // CHUNK,)),
        ],
        compiler_params=params(FULL_VMEM_BYTES),
        name="gate",
    )(fwd_proj, rev_proj, tokens.reshape(1, rows), short_taps)


    me = lax.axis_index("ctx").astype(jnp.int32).reshape(1)
    sent, me = lax.optimization_barrier((sent, me))
    received = exchange(sent)
    section_shape = jax.ShapeDtypeStruct((PAIRS, 2 * inner, lanes), jnp.bfloat16)
    spectrum_cost = cost(3 * PAIRS * 2 * (2 * inner) ** 2 * lanes, 4 * 1024 * 1024)
    high, low, own_taps, own_core, own_phases = pl.pallas_call(
        sections_kernel,
        out_shape=(
            section_shape,
            section_shape,
            jax.ShapeDtypeStruct((8, lanes), jnp.float32),
            jax.ShapeDtypeStruct(core.shape[1:], jnp.float32),
            jax.ShapeDtypeStruct(phases.shape, jnp.float32),
        ),
        in_specs=[SMEM] + [HBM] * 5,
        out_specs=(VMEM,) * 5,
        scratch_shapes=[
            pltpu.VMEM((count, length), jnp.float32),
            pltpu.VMEM((1, count), jnp.float32),
            pltpu.VMEM(short_taps.shape, jnp.float32),
            pltpu.VMEM(core.shape, jnp.float32),
            pltpu.VMEM((2,) + outer_shape, jnp.bfloat16),
            pltpu.VMEM((PAIRS, 2, inner, lanes), jnp.float32),
            pltpu.VMEM((HALF, per, half_rows, lanes), jnp.float32),
            pltpu.SemaphoreType.DMA((6,)),
        ],
        compiler_params=params(),
        cost_estimate=spectrum_cost,
        name="sections",
    )(me, long_kernel, skip_gain.reshape(1, count), short_taps, core, phases)

    own_taps, fwd_o, rev_o = lax.optimization_barrier((own_taps, fwd_o, rev_o))
    fwd_o = shifted(fwd_o, 1)
    rev_o = shifted(rev_o, -1)
    own_taps, fwd_o, rev_o = lax.optimization_barrier((own_taps, fwd_o, rev_o))

    groups = [min(BIN_GROUP, BINS - first) for first in range(0, BINS, BIN_GROUP)]
    spectrum = pl.pallas_call(
        spectrum_kernel,
        out_shape=tuple(
            jax.ShapeDtypeStruct((group, 2 * inner, lanes), jnp.float32) for group in groups
        )
        + (jax.ShapeDtypeStruct(mix.shape[1:], jnp.bfloat16),),
        in_specs=[VMEM, VMEM, HBM],
        out_specs=(VMEM,) * (len(groups) + 1),
        scratch_shapes=[
            pltpu.VMEM(mix.shape, jnp.bfloat16),
            pltpu.SemaphoreType.DMA((2,)),
        ],
        compiler_params=params(),
        cost_estimate=spectrum_cost,
        name="spectrum",
    )(high, low, mix)

    filtered = pl.pallas_call(
        filter_kernel,
        out_shape=jax.ShapeDtypeStruct((HALF, per, rows, lanes), jnp.bfloat16),
        in_specs=[VMEM] * (4 + len(spectrum)),
        out_specs=VMEM,
        scratch_shapes=[
            pltpu.VMEM((BINS, 2 * inner, lanes), jnp.bfloat16),
            pltpu.VMEM((OUTER, inner, lanes), jnp.bfloat16),
            pltpu.VMEM(outer_shape, jnp.bfloat16),
        ],
        compiler_params=params(),
        cost_estimate=cost(4 * PAIRS * 4 * (2 * inner) ** 2 * lanes, 4 * 1024 * 1024),
        name="filter",
    )(received.reshape(HALF, per, padded, lanes), own_taps, own_core, own_phases, *spectrum)

    returned = exchange(filtered.reshape(devices, rows, lanes))

    return pl.pallas_call(
        mixing_kernel,
        out_shape=jax.ShapeDtypeStruct((rows, width), jnp.bfloat16),
        in_specs=[VMEM] * 7,
        out_specs=VMEM,
        scratch_shapes=[
            pltpu.VMEM((rows, width), jnp.bfloat16),
            pltpu.VMEM((rows, width), jnp.float32),
        ],
        compiler_params=params(),
        cost_estimate=cost(2 * rows * width * width, 4 * 1024 * 1024),
        name="mixing",
    )(returned, fwd_o, rev_o, fwd_proj, rev_proj, short_taps, out_weight)


def solution(mesh):
    in_specs = (
        P(("dp", "ctx"), None),
        P(("dp", "ctx"), None),
        P(("dp", "ctx")),
        P(),
        P("ctx", None),
        P("ctx"),
        P(),
    )
    out_specs = P(("dp", "ctx"), None)
    return jax.shard_map(
        per_device, mesh=mesh, in_specs=in_specs, out_specs=out_specs, check_vma=False
    )
```

time: 124 us -> 50.3 us (0.41)
  local copies, waits for them, and re-layouts: 38 us -> 1.98 us
  matrix products: 32.3 us -> 0 us
  other arithmetic: 13.8 us -> 0 us
  Pallas kernels: 0 us -> 11.1 us
  starting transfers between devices: 13 us -> 11.1 us
    dot_general x23 -> x0, matrix products: 32.3 us -> none  [the longest x12 18.5 us: right_product(): jnp.einsum('ckn,nm->ckm', signal, matrix, precision=lax.Precision.HIGHEST)]
    unnamed x32 -> x26, local copies, waits for them, and re-layouts: 13.5 us -> 1.98 us
    rev x3 -> x0, local copies, waits for them, and re-layouts: 11.4 us -> none  [the longest x1 6.47 us: per_device(): rev_out = jnp.flip(rev_flipped, 1).astype(jnp.bfloat16)]
    pallas_call x0 -> x5, Pallas kernels: none -> 11.1 us  [the longest x1 3.42 us: per_device(): pl.pallas_call(gate_kernel, out_shape=(jax.ShapeDtypeStruct(block, jnp.bf...]
    convert_element_type x4 -> x0, other arithmetic: 6.48 us -> none  [the longest x1 3.62 us: per_device(): fwd_ext = jnp.concatenate([low_rows, fwd_proj], axis=0).astype(jnp.float32)]
    add x2 -> x0, other arithmetic: 4.08 us -> none  [the longest x1 3.17 us: per_device(): short_taps[0] * fwd_ext[2:] + short_taps[1] * fwd_ext[1:-1]]
    another operation x2 -> x0, local copies, waits for them, and re-layouts: 3.69 us -> none  [the longest x1 2.34 us: per_device(): stacked = jnp.stack([fwd_out, rev_out], axis=1)]
    all_to_all x3 -> x0, local copies, waits for them, and re-layouts: 3.08 us -> none  [the longest x1 1.85 us: per_device(): lax.all_to_all(stacked, 'ctx', split_axis=2, concat_axis=0, tiled=True)]
  transfers between devices with their start and end apart: 3 -> 3, of which waited for: 1 -> 2; matrix products, arithmetic and copies ran while one was open for 19% -> 0% of each run, Pallas kernels for 0% -> 7%
where the time goes in v1:
time: 50.3 us; the launch traced here: 49.9 us
  blocking collectives  18.5 us (37%)
  Pallas kernels  11.1 us (22%)
  starting transfers between devices  11.1 us (22%)
  waiting for transfers between devices  7.08 us (14%)
  local copies, waits for them, and re-layouts  1.98 us (4%)
    all_to_all x1, blocking collectives, exchange(): return lax.all_to_all(value, 'ctx', split_axis=0, concat_axis=0, tiled=True)  18.5 us
    all_to_all x1, starting transfers between devices, exchange(): return lax.all_to_all(value, 'ctx', split_axis=0, concat_axis=0, tiled=True)  7.54 us
    all_to_all x1, waiting for transfers between devices, exchange(): return lax.all_to_all(value, 'ctx', split_axis=0, concat_axis=0, tiled=True)  6.03 us
    ppermute x2, starting transfers between devices, shifted(): lax.ppermute(value, 'ctx', [(source, source + steps) for source in range(...  3.6 us
    pallas_call x1, Pallas kernels, per_device(): pl.pallas_call(gate_kernel, out_shape=(jax.ShapeDtypeStruct(block, jnp.bf...  3.42 us
    pallas_call x1, Pallas kernels, per_device(): pl.pallas_call(filter_kernel, out_shape=jax.ShapeDtypeStruct((HALF, per,...  2.61 us
    pallas_call x1, Pallas kernels, per_device(): pl.pallas_call(sections_kernel, out_shape=(section_shape, section_shape,...  2.39 us
    unnamed x26, local copies, waits for them, and re-layouts  1.98 us
  transfers between devices with their start and end apart: 3, of which 2 were waited for; matrix products, arithmetic and copies ran while one was open for 0% of the time, Pallas kernels for 7%

profile of v1, /device:TPU:0, one launch (start us, length us, event | category | flops | bytes accessed | tf_op | source)
XLA Modules:
  0.0 49.9 jit_solution(3204542482943049775)
XLA Ops:
  0.0 0.0 copy-start.7
  0.0 0.0 copy-start.8
  0.0 0.0 copy-start.3
  0.0 0.0 copy-start.5
  0.0 0.0 copy-start.4
  0.0 0.0 copy-start.6
  0.0 3.4 %gate.1 = (bf16[16,136,128]{2,1,0:T(8,128)(2,1)}, f32[8,256]{1,0:T(8,128)}, f32[8,256]{1,0:T(8,128)}) custom-call(bf16[128,3072]{1,0:T(8,128)(2,1)} %fwd_ref.1, bf16[128,3072]{1,0:T(8,128)(2,1)} %rev_ref.1, s32[1,128]{1,0:T(1,128)} %bitcast.8, f32[3,3072]{1,0:T(4,128)} %taps_ref.1), custom_call_target="tpu_custom_call" | custom-call | tf_op jit(solution)/shard_map/gate/pallas_call | solution.py:655
  3.5 0.0 copy-start.12
  3.5 0.0 copy-start.11
  3.5 7.5 %all-to-all-start = ((bf16[16,136,128]{2,1,0:T(8,128)(2,1)}), bf16[16,136,128]{2,1,0:T(8,128)(2,1)S(1)}, u32[]{:S(2)}, u32[]{:S(2)}) async-start(bf16[16,136,128]{2,1,0:T(8,128)(2,1)} %get-tuple-element.26), calls=%async_computation | async-start | bytes 1114112 | tf_op jit(solution)/shard_map/all_to_all | solution.py:630
  11.0 0.0 copy-done.7
  11.0 0.0 copy-done.8
  11.1 0.0 copy-done.3
  11.1 0.0 copy-done.5
  11.1 0.0 copy-done.4
  11.1 2.4 %sections.1 = (bf16[9,256,128]{2,1,0:T(8,128)(2,1)S(1)}, bf16[9,256,128]{2,1,0:T(8,128)(2,1)S(1)}, f32[8,128]{1,0:T(8,128)S(1)}, f32[32,256]{1,0:T(8,128)S(1)}, f32[128,128]{1,0:T(8,128)S(1)}) custom-call(s32[1]{0:T(128)} %bitcast.1.me_ref, f32[64,2048]{1,0:T(8,128)S(1)} %copy-done.4, f32[1,64]{1,0:T(1,128)S(1)} %bitcast.7, f32[3,3072]{1,0:T(4,128)S(1)} %copy-done.3, ...), custom_call_target="tpu_custom_call" | custom-call | flops 452984832 | bytes 4194304 | tf_op jit(solution)/shard_map/sections/pallas_call | solution.py:689
  13.5 0.0 copy-done.12
  13.5 2.3 %collective-permute-start = (f32[8,256]{1,0:T(8,128)S(1)}, f32[8,256]{1,0:T(8,128)S(1)}, u32[]{:S(2)}, u32[]{:S(2)}) collective-permute-start(f32[8,256]{1,0:T(8,128)S(1)} %copy-done.12), channel_id=1, source_target_pairs={{0,1},{1,2},{2,3},{3,4},{4,5},{5,6},{6,7},{7,8},{8,9},{9,10},{10,1... | collective-permute-start | bytes 24584 | tf_op jit(solution)/shard_map/ppermute | solution.py:636
  15.8 0.0 copy-done.11
  15.8 1.3 %collective-permute-start.1 = (f32[8,256]{1,0:T(8,128)S(1)}, f32[8,256]{1,0:T(8,128)S(1)}, u32[]{:S(2)}, u32[]{:S(2)}) collective-permute-start(f32[8,256]{1,0:T(8,128)S(1)} %copy-done.11), channel_id=1, source_target_pairs={{1,0},{2,1},{3,2},{4,3},{5,4},{6,5},{7,6},{8,7},{9,8},{10,9},{11,1... | collective-permute-start | bytes 24584 | tf_op jit(solution)/shard_map/ppermute | solution.py:636
  17.1 0.0 copy-done.6
  17.1 1.0 %spectrum.1 = (f32[6,256,128]{2,1,0:T(8,128)S(1)}, f32[6,256,128]{2,1,0:T(8,128)S(1)}, f32[5,256,128]{2,1,0:T(8,128)S(1)}, bf16[256,256]{1,0:T(8,128)(2,1)S(1)}) custom-call(bf16[9,256,128]{2,1,0:T(8,128)(2,1)S(1)} %get-tuple-element.37.high, bf16[9,256,128]{2,1,0:T(8,128)(2,1)S(1)} %get-tuple-element.38.low, bf16[2,256,256]{2,1,0:T(8,128)(2,1)S(1)} %copy-done.6), custom_call_target="tpu_custom_call" | custom-call | flops 452984832 | bytes 4194304 | tf_op jit(solution)/shard_map/spectrum/pallas_call | solution.py:721
  18.1 0.0 copy-start.9
  18.1 0.8 %copy-done.9 = f32[5,256,128]{2,1,0:T(8,128)} copy-done((f32[5,256,128]{2,1,0:T(8,128)}, f32[5,256,128]{2,1,0:T(8,128)S(1)}, u32[]{:S(2)}) %copy-start.9) | copy-done | bytes 655384
  19.0 0.0 collective-permute-done.fwd_o_ref
  19.0 1.1 %collective-permute-done.1.rev_o_ref = f32[8,256]{1,0:T(8,128)S(1)} collective-permute-done((f32[8,256]{1,0:T(8,128)S(1)}, f32[8,256]{1,0:T(8,128)S(1)}, u32[]{:S(2)}, u32[]{:S(2)}) %collective-permute-start.1) | collective-permute-done | bytes 8224 | tf_op jit(solution)/shard_map/ppermute | solution.py:636
  20.0 6.0 %all-to-all-done = bf16[16,136,128]{2,1,0:T(8,128)(2,1)S(1)} async-done(((bf16[16,136,128]{2,1,0:T(8,128)(2,1)}), bf16[16,136,128]{2,1,0:T(8,128)(2,1)S(1)}, u32[]{:S(2)}, u32[]{:S(2)}) %all-to-all-start) | async-done | bytes 557088 | tf_op jit(solution)/shard_map/all_to_all | solution.py:630
  26.1 0.0 copy-start.10
  26.1 1.1 %copy-done.10 = f32[5,256,128]{2,1,0:T(8,128)S(1)} copy-done((f32[5,256,128]{2,1,0:T(8,128)S(1)}, f32[5,256,128]{2,1,0:T(8,128)}, u32[]{:S(2)}) %copy-start.10) | copy-done | bytes 655384
  27.1 0.0 copy-start
  27.1 0.0 copy-start.1
  27.1 0.0 copy-start.2
  27.1 2.6 %filter.1 = bf16[16,1,128,128]{3,2,1,0:T(8,128)(2,1)S(1)} custom-call(bf16[16,1,136,128]{3,2,1,0:T(8,128)(2,1)S(1)} %bitcast.5, f32[8,128]{1,0:T(8,128)S(1)} %get-tuple-element.34.own_taps_ref, f32[32,256]{1,0:T(8,128)S(1)} %get-tuple-element.35.core_ref, f32[128,128]{1,0:T(8,128)S(1)} %get-tuple-element.36.turn_ref, ...), custom_call_target="tpu_custom_call" | custom-call | flops 1207959552 | bytes 4194304 | tf_op jit(solution)/shard_map/filter/pallas_call | solution.py:738
  29.8 18.5 %all_to_all.10.ret_ref = bf16[16,128,128]{2,1,0:T(8,128)(2,1)S(1)} all-to-all(bf16[16,128,128]{2,1,0:T(8,128)(2,1)S(1)} %bitcast.6), channel_id=1, replica_groups=mesh['dp'=2,'ctx'=16] {'ctx'}, dimensions={0} | all-to-all | bytes 1048576 | tf_op jit(solution)/shard_map/all_to_all | solution.py:630
  48.3 0.0 copy-done
  48.3 0.0 copy-done.1
  48.3 0.0 copy-done.2
  48.3 1.7 %mixing.1 = bf16[128,1024]{1,0:T(8,128)(2,1)} custom-call(bf16[16,128,128]{2,1,0:T(8,128)(2,1)S(1)} %all_to_all.10.ret_ref, f32[8,256]{1,0:T(8,128)S(1)} %collective-permute-done.fwd_o_ref, f32[8,256]{1,0:T(8,128)S(1)} %collective-permute-done.1.rev_o_ref, bf16[128,3072]{1,0:T(8,128)(2,1)S(1)} %copy-done, bf16[128,3072]{1,0:T(8,128)(2,1)S(1)} %copy-done.1, ...), custom_call_target="tpu_custom_call" | custom-call | flops 268435456 | bytes 4194304 | tf_op jit(solution)/shard_map/mixing/pallas_call | solution.py:755
Async XLA Ops:
  0.0 11.0 %copy-start.7 = (f32[128,128]{1,0:T(8,128)S(1)}, f32[128,128]{1,0:T(8,128)}, u32[]{:S(2)}) copy-start(f32[128,128]{1,0:T(8,128)} %constant.12.clone.phase_hbm) | copy-start | bytes 196612
  0.0 11.0 %copy-start.8 = (f32[2,32,256]{2,1,0:T(8,128)S(1)}, f32[2,32,256]{2,1,0:T(8,128)}, u32[]{:S(2)}) copy-start(f32[2,32,256]{2,1,0:T(8,128)} %constant.10.clone.core_hbm) | copy-start | bytes 196612
  0.0 11.0 %copy-start.3 = (f32[3,3072]{1,0:T(4,128)S(1)}, f32[3,3072]{1,0:T(4,128)}, u32[]{:S(2)}) copy-start(f32[3,3072]{1,0:T(4,128)} %taps_ref.1) | copy-start | bytes 110596
  0.0 11.1 %copy-start.5 = (f32[64]{0:T(128)S(1)}, f32[64]{0:T(128)}, u32[]{:S(2)}) copy-start(f32[64]{0:T(128)} %param.15) | copy-start | bytes 772
  0.0 11.1 %copy-start.4 = (f32[64,2048]{1,0:T(8,128)S(1)}, f32[64,2048]{1,0:T(8,128)}, u32[]{:S(2)}) copy-start(f32[64,2048]{1,0:T(8,128)} %kernel_hbm.1) | copy-start | bytes 1572868
  0.0 17.1 %copy-start.6 = (bf16[2,256,256]{2,1,0:T(8,128)(2,1)S(1)}, bf16[2,256,256]{2,1,0:T(8,128)(2,1)}, u32[]{:S(2)}) copy-start(bf16[2,256,256]{2,1,0:T(8,128)(2,1)} %constant.11.clone.mix_hbm) | copy-start | bytes 786436
  3.5 10.0 %copy-start.12 = (f32[8,256]{1,0:T(8,128)S(1)}, f32[8,256]{1,0:T(8,128)}, u32[]{:S(2)}) copy-start(f32[8,256]{1,0:T(8,128)} %get-tuple-element.32) | copy-start | bytes 24580
  3.5 12.3 %copy-start.11 = (f32[8,256]{1,0:T(8,128)S(1)}, f32[8,256]{1,0:T(8,128)}, u32[]{:S(2)}) copy-start(f32[8,256]{1,0:T(8,128)} %get-tuple-element.33) | copy-start | bytes 24580
  3.5 22.6 %all-to-all-start = ((bf16[16,136,128]{2,1,0:T(8,128)(2,1)}), bf16[16,136,128]{2,1,0:T(8,128)(2,1)S(1)}, u32[]{:S(2)}, u32[]{:S(2)}) async-start(bf16[16,136,128]{2,1,0:T(8,128)(2,1)} %get-tuple-element.26), calls=%async_computation | async-start | bytes 1114112 | tf_op jit(solution)/shard_map/all_to_all | solution.py:630
  13.5 5.5 %collective-permute-start = (f32[8,256]{1,0:T(8,128)S(1)}, f32[8,256]{1,0:T(8,128)S(1)}, u32[]{:S(2)}, u32[]{:S(2)}) collective-permute-start(f32[8,256]{1,0:T(8,128)S(1)} %copy-done.12), channel_id=1, source_target_pairs={{0,1},{1,2},{2,3},{3,4},{4,5},{5,6},{6,7},{7,8},{8,9},{9,10},{10,1... | collective-permute-start | bytes 24584 | tf_op jit(solution)/shard_map/ppermute | solution.py:636
  15.8 4.2 %collective-permute-start.1 = (f32[8,256]{1,0:T(8,128)S(1)}, f32[8,256]{1,0:T(8,128)S(1)}, u32[]{:S(2)}, u32[]{:S(2)}) collective-permute-start(f32[8,256]{1,0:T(8,128)S(1)} %copy-done.11), channel_id=1, source_target_pairs={{1,0},{2,1},{3,2},{4,3},{5,4},{6,5},{7,6},{8,7},{9,8},{10,9},{11,1... | collective-permute-start | bytes 24584 | tf_op jit(solution)/shard_map/ppermute | solution.py:636
  18.1 0.9 %copy-start.9 = (f32[5,256,128]{2,1,0:T(8,128)}, f32[5,256,128]{2,1,0:T(8,128)S(1)}, u32[]{:S(2)}) copy-start(f32[5,256,128]{2,1,0:T(8,128)S(1)} %get-tuple-element.41.refs_2_) | copy-start | bytes 1966084
  26.1 1.1 %copy-start.10 = (f32[5,256,128]{2,1,0:T(8,128)S(1)}, f32[5,256,128]{2,1,0:T(8,128)}, u32[]{:S(2)}) copy-start(f32[5,256,128]{2,1,0:T(8,128)} %copy-done.9) | copy-start | bytes 1966084
  27.1 21.1 %copy-start = (bf16[128,3072]{1,0:T(8,128)(2,1)S(1)}, bf16[128,3072]{1,0:T(8,128)(2,1)}, u32[]{:S(2)}) copy-start(bf16[128,3072]{1,0:T(8,128)(2,1)} %fwd_ref.1) | copy-start | bytes 2359300
  27.1 21.1 %copy-start.1 = (bf16[128,3072]{1,0:T(8,128)(2,1)S(1)}, bf16[128,3072]{1,0:T(8,128)(2,1)}, u32[]{:S(2)}) copy-start(bf16[128,3072]{1,0:T(8,128)(2,1)} %rev_ref.1) | copy-start | bytes 2359300
  27.1 21.1 %copy-start.2 = (bf16[1024,1024]{1,0:T(8,128)(2,1)S(1)}, bf16[1024,1024]{1,0:T(8,128)(2,1)}, u32[]{:S(2)}) copy-start(bf16[1024,1024]{1,0:T(8,128)(2,1)} %weight_ref.1) | copy-start | bytes 6291460

commit v2 on v1

--- a/solution.py
+++ b/solution.py
@@ -17,7 +17,7 @@
 LANES = 128
 TILE = 16
 CHUNK = 32
-BIN_GROUP = 6
+BIN_GROUP = 2
 VMEM_BYTES = 30 * 1024 * 1024
 EDGE_LANES = 256
 EDGE_ROWS = 2
@@ -151,11 +151,13 @@
     return cos, sin
 
 
-def store_sections(section, turn_ref, tile, lanes, put):
+def store_sections(section, turn_ref, wide_ref, tile, lanes, put):
     start = tile * TILE
     by_row = section.reshape(OUTER, TILE, lanes)
     for bin_index in range(BINS):
         cos, sin = turn_pair(turn_ref, start, TILE, bin_index, lanes)
+        wide_ref[bin_index, 0, start : start + TILE, :] = cos
+        wide_ref[bin_index, 1, start : start + TILE, :] = sin
         if bin_index in (0, HALF):
             real = by_row[0 if bin_index == 0 else 1]
             put(bin_index, start, real * cos, real * -sin)
@@ -217,18 +219,24 @@
     ]
     loads, stores = [], []
     for step in range(rows // CHUNK):
-        part = (pl.ds(step * CHUNK, CHUNK), pl.ds(0, 2 * width))
+        start, end = step * CHUNK, (step + 1) * CHUNK
+        rev_start = start + TILE if step else 0
+        rev_end = min(end + TILE, rows)
+        part = (pl.ds(start, CHUNK), pl.ds(0, 2 * width))
+        rev_part = (pl.ds(rev_start, rev_end - rev_start), pl.ds(0, 2 * width))
         copies = [
             pltpu.make_async_copy(fwd_hbm.at[part], fwd_ref.at[part], sems.at[step, 0]),
-            pltpu.make_async_copy(rev_hbm.at[part], rev_ref.at[part], sems.at[step, 1]),
+            pltpu.make_async_copy(rev_hbm.at[rev_part], rev_ref.at[rev_part], sems.at[step, 1]),
         ]
         for copy in copies:
             copy.start()
         loads.append(copies)
         if step == 0:
-            for copy in small:
+            for copy in small[:2]:
                 copy.start()
-    for copy in small:
+    for copy in small[2:]:
+        copy.start()
+    for copy in small[:2]:
         copy.wait()
     known_row = jnp.where(tokens_ref[...] != 4, 1.0, 0.0).astype(jnp.float32)
     known = jnp.transpose(jnp.broadcast_to(known_row, (LANES, rows)))
@@ -249,14 +257,11 @@
         return jnp.where((edge_row >= rows_at) & (edge_row < rows_at + 2), moved, edge)
 
     pieces = LANES // count
-    for copy in loads[0]:
-        copy.wait()
     for step in range(rows // CHUNK):
         start = step * CHUNK
         final = start + CHUNK == rows
-        if not final:
-            for copy in loads[step + 1]:
-                copy.wait()
+        for copy in loads[step] + (small[2:] if final else []):
+            copy.wait()
         here = slice(start, start + CHUNK)
         for block in range(width // LANES):
             low = block * LANES
@@ -469,7 +474,7 @@
 
 
 def filter_kernel(recv_ref, own_taps_ref, core_ref, turn_ref, *refs):
-    *spec_refs, mix_ref, out_ref, sections, returned, enter_ref = refs
+    *spec_refs, mix_ref, out_ref, sections, returned, enter_ref, wide_ref = refs
     expand(core_ref[...], enter_ref)
     blocks, per, padded, lanes = recv_ref.shape
     rows = padded - EXTRA
@@ -490,14 +495,15 @@
         def section_of(tile):
             return dot(enter_ref[...], jnp.concatenate(loaded[tile : tile + 2], axis=1))
 
-        ahead = section_of(0)
-        for tile in range(0, tiles, 2):
+        order = list(range(2, tiles - 2, 2)) + [0, tiles - 2]
+        ahead = section_of(order[0])
+        for place, tile in enumerate(order):
             section = ahead
-            if tile + 2 < tiles:
-                ahead = section_of(tile + 2)
+            if place + 1 < len(order):
+                ahead = section_of(order[place + 1])
             at = group * tiles + tile
-            store_sections(section[:, :lanes], turn_ref, at, lanes, put)
-            store_sections(section[:, lanes:], turn_ref, at + 1, lanes, put)
+            store_sections(section[:, :lanes], turn_ref, wide_ref, at, lanes, put)
+            store_sections(section[:, lanes:], turn_ref, wide_ref, at + 1, lanes, put)
 
     def bins_from(first):
         return range(first, min(first + 2, BINS))
@@ -520,7 +526,7 @@
         for at, b in enumerate(bins_from(first)):
             real = back[:inner, at * lanes : (at + 1) * lanes]
             imag = back[inner:, at * lanes : (at + 1) * lanes]
-            cos, sin = turn_pair(turn_ref, 0, inner, b, lanes)
+            cos, sin = wide_ref[b, 0], wide_ref[b, 1]
             returned[slot(b, 0)] = (real * cos + imag * sin).astype(jnp.bfloat16)
             if b not in (0, HALF):
                 returned[slot(b, 1)] = (real * sin - imag * cos).astype(jnp.bfloat16)
@@ -744,6 +750,7 @@
             pltpu.VMEM((BINS, 2 * inner, lanes), jnp.bfloat16),
             pltpu.VMEM((OUTER, inner, lanes), jnp.bfloat16),
             pltpu.VMEM(outer_shape, jnp.bfloat16),
+            pltpu.VMEM((BINS, 2, inner, lanes), jnp.float32),
         ],
         compiler_params=params(),
         cost_estimate=cost(4 * PAIRS * 4 * (2 * inner) ** 2 * lanes, 4 * 1024 * 1024),

time: 50.3 us -> 48.9 us (0.972)
  local copies, waits for them, and re-layouts: 1.98 us -> 0.05 us
  waiting for transfers between devices: 7.08 us -> 7.93 us
    unnamed x26 -> x22, local copies, waits for them, and re-layouts: 1.98 us -> 0.05 us
    ppermute x2, waiting for transfers between devices: 1.06 us -> 1.9 us  [shifted(): lax.ppermute(value, 'ctx', [(source, source + steps) for source in range(...]
where the time goes in v2:
time: 48.9 us; the launch traced here: 48.5 us
  blocking collectives  18.5 us (38%)
  starting transfers between devices  11.1 us (23%)
  Pallas kernels  10.7 us (22%)
  waiting for transfers between devices  7.93 us (16%)
    all_to_all x1, blocking collectives, exchange(): return lax.all_to_all(value, 'ctx', split_axis=0, concat_axis=0, tiled=True)  18.5 us
    all_to_all x1, starting transfers between devices, exchange(): return lax.all_to_all(value, 'ctx', split_axis=0, concat_axis=0, tiled=True)  7.54 us
    all_to_all x1, waiting for transfers between devices, exchange(): return lax.all_to_all(value, 'ctx', split_axis=0, concat_axis=0, tiled=True)  6.03 us
    ppermute x2, starting transfers between devices, shifted(): lax.ppermute(value, 'ctx', [(source, source + steps) for source in range(...  3.6 us
    pallas_call x1, Pallas kernels, per_device(): pl.pallas_call(gate_kernel, out_shape=(jax.ShapeDtypeStruct(block, jnp.bf...  3.38 us
    pallas_call x1, Pallas kernels, per_device(): pl.pallas_call(sections_kernel, out_shape=(section_shape, section_shape,...  2.39 us
    pallas_call x1, Pallas kernels, per_device(): pl.pallas_call(filter_kernel, out_shape=jax.ShapeDtypeStruct((HALF, per,...  2.32 us
    ppermute x2, waiting for transfers between devices, shifted(): lax.ppermute(value, 'ctx', [(source, source + steps) for source in range(...  1.9 us
  transfers between devices with their start and end apart: 3, of which 2 were waited for; matrix products, arithmetic and copies ran while one was open for 0% of the time, Pallas kernels for 7%

profile of v2, /device:TPU:0, one launch (start us, length us, event | category | flops | bytes accessed | tf_op | source)
XLA Modules:
  0.0 48.5 jit_solution(8957886909335358616)
XLA Ops:
  0.0 0.0 copy-start.7
  0.0 0.0 copy-start.8
  0.0 0.0 copy-start.3
  0.0 0.0 copy-start.5
  0.0 0.0 copy-start.4
  0.0 0.0 copy-start.6
  0.0 3.4 %gate.1 = (bf16[16,136,128]{2,1,0:T(8,128)(2,1)}, f32[8,256]{1,0:T(8,128)}, f32[8,256]{1,0:T(8,128)}) custom-call(bf16[128,3072]{1,0:T(8,128)(2,1)} %fwd_ref.1, bf16[128,3072]{1,0:T(8,128)(2,1)} %rev_ref.1, s32[1,128]{1,0:T(1,128)} %bitcast.8, f32[3,3072]{1,0:T(4,128)} %taps_ref.1), custom_call_target="tpu_custom_call" | custom-call | tf_op jit(solution)/shard_map/gate/pallas_call | solution.py:661
  3.4 0.0 copy-start.10
  3.4 0.0 copy-start.9
  3.4 7.5 %all-to-all-start = ((bf16[16,136,128]{2,1,0:T(8,128)(2,1)}), bf16[16,136,128]{2,1,0:T(8,128)(2,1)S(1)}, u32[]{:S(2)}, u32[]{:S(2)}) async-start(bf16[16,136,128]{2,1,0:T(8,128)(2,1)} %get-tuple-element.32), calls=%async_computation | async-start | bytes 1114112 | tf_op jit(solution)/shard_map/all_to_all | solution.py:636
  11.0 0.0 copy-done.7
  11.0 0.0 copy-done.8
  11.0 0.0 copy-done.3
  11.0 0.0 copy-done.5
  11.0 0.0 copy-done.4
  11.0 2.4 %sections.1 = (bf16[9,256,128]{2,1,0:T(8,128)(2,1)S(1)}, bf16[9,256,128]{2,1,0:T(8,128)(2,1)S(1)}, f32[8,128]{1,0:T(8,128)S(1)}, f32[32,256]{1,0:T(8,128)S(1)}, f32[128,128]{1,0:T(8,128)S(1)}) custom-call(s32[1]{0:T(128)} %bitcast.1.me_ref, f32[64,2048]{1,0:T(8,128)S(1)} %copy-done.4, f32[1,64]{1,0:T(1,128)S(1)} %bitcast.7, f32[3,3072]{1,0:T(4,128)S(1)} %copy-done.3, ...), custom_call_target="tpu_custom_call" | custom-call | flops 452984832 | bytes 4194304 | tf_op jit(solution)/shard_map/sections/pallas_call | solution.py:695
  13.4 0.0 copy-done.10
  13.5 2.3 %collective-permute-start = (f32[8,256]{1,0:T(8,128)S(1)}, f32[8,256]{1,0:T(8,128)S(1)}, u32[]{:S(2)}, u32[]{:S(2)}) collective-permute-start(f32[8,256]{1,0:T(8,128)S(1)} %copy-done.10), channel_id=1, source_target_pairs={{0,1},{1,2},{2,3},{3,4},{4,5},{5,6},{6,7},{7,8},{8,9},{9,10},{10,1... | collective-permute-start | bytes 24584 | tf_op jit(solution)/shard_map/ppermute | solution.py:642
  15.8 0.0 copy-done.9
  15.8 1.3 %collective-permute-start.1 = (f32[8,256]{1,0:T(8,128)S(1)}, f32[8,256]{1,0:T(8,128)S(1)}, u32[]{:S(2)}, u32[]{:S(2)}) collective-permute-start(f32[8,256]{1,0:T(8,128)S(1)} %copy-done.9), channel_id=1, source_target_pairs={{1,0},{2,1},{3,2},{4,3},{5,4},{6,5},{7,6},{8,7},{9,8},{10,9},{11,1... | collective-permute-start | bytes 24584 | tf_op jit(solution)/shard_map/ppermute | solution.py:642
  17.1 0.0 copy-done.6
  17.1 1.0 %spectrum.1 = (f32[2,256,128]{2,1,0:T(8,128)S(1)}, f32[2,256,128]{2,1,0:T(8,128)S(1)}, f32[2,256,128]{2,1,0:T(8,128)S(1)}, f32[2,256,128]{2,1,0:T(8,128)S(1)}, f...) custom-call(bf16[9,256,128]{2,1,0:T(8,128)(2,1)S(1)} %get-tuple-elem, ...), custom_call_target="tpu_custom_call" | custom-call | flops 452984832 | bytes 4194304 | tf_op jit(solution)/shard_map/spectrum/pallas_call | solution.py:727
  18.1 0.0 collective-permute-done.fwd_o_ref
  18.1 1.9 %collective-permute-done.1.rev_o_ref = f32[8,256]{1,0:T(8,128)S(1)} collective-permute-done((f32[8,256]{1,0:T(8,128)S(1)}, f32[8,256]{1,0:T(8,128)S(1)}, u32[]{:S(2)}, u32[]{:S(2)}) %collective-permute-start.1) | collective-permute-done | bytes 8224 | tf_op jit(solution)/shard_map/ppermute | solution.py:642
  20.0 6.0 %all-to-all-done = bf16[16,136,128]{2,1,0:T(8,128)(2,1)S(1)} async-done(((bf16[16,136,128]{2,1,0:T(8,128)(2,1)}), bf16[16,136,128]{2,1,0:T(8,128)(2,1)S(1)}, u32[]{:S(2)}, u32[]{:S(2)}) %all-to-all-start) | async-done | bytes 557088 | tf_op jit(solution)/shard_map/all_to_all | solution.py:636
  26.0 0.0 copy-start
  26.0 0.0 copy-start.1
  26.0 0.0 copy-start.2
  26.0 2.3 %filter.1 = bf16[16,1,128,128]{3,2,1,0:T(8,128)(2,1)S(1)} custom-call(bf16[16,1,136,128]{3,2,1,0:T(8,128)(2,1)S(1)} %bitcast.5, f32[8,128]{1,0:T(8,128)S(1)} %get-tuple-element.40.own_taps_ref, f32[32,256]{1,0:T(8,128)S(1)} %get-tuple-element.41.core_ref, f32[128,128]{1,0:T(8,128)S(1)} %get-tuple-element.42.turn_ref, ...), custom_call_target="tpu_custom_call" | custom-call | flops 1207959552 | bytes 4194304 | tf_op jit(solution)/shard_map/filter/pallas_call | solution.py:744
  28.3 18.5 %all_to_all.10.ret_ref = bf16[16,128,128]{2,1,0:T(8,128)(2,1)S(1)} all-to-all(bf16[16,128,128]{2,1,0:T(8,128)(2,1)S(1)} %bitcast.6), channel_id=1, replica_groups=mesh['dp'=2,'ctx'=16] {'ctx'}, dimensions={0} | all-to-all | bytes 1048576 | tf_op jit(solution)/shard_map/all_to_all | solution.py:636
  46.9 0.0 copy-done
  46.9 0.0 copy-done.1
  46.9 0.0 copy-done.2
  46.9 1.7 %mixing.1 = bf16[128,1024]{1,0:T(8,128)(2,1)} custom-call(bf16[16,128,128]{2,1,0:T(8,128)(2,1)S(1)} %all_to_all.10.ret_ref, f32[8,256]{1,0:T(8,128)S(1)} %collective-permute-done.fwd_o_ref, f32[8,256]{1,0:T(8,128)S(1)} %collective-permute-done.1.rev_o_ref, bf16[128,3072]{1,0:T(8,128)(2,1)S(1)} %copy-done, bf16[128,3072]{1,0:T(8,128)(2,1)S(1)} %copy-done.1, ...), custom_call_target="tpu_custom_call" | custom-call | flops 268435456 | bytes 4194304 | tf_op jit(solution)/shard_map/mixing/pallas_call | solution.py:762
Async XLA Ops:
  0.0 11.0 %copy-start.7 = (f32[128,128]{1,0:T(8,128)S(1)}, f32[128,128]{1,0:T(8,128)}, u32[]{:S(2)}) copy-start(f32[128,128]{1,0:T(8,128)} %constant.12.clone.phase_hbm) | copy-start | bytes 196612
  0.0 11.0 %copy-start.8 = (f32[2,32,256]{2,1,0:T(8,128)S(1)}, f32[2,32,256]{2,1,0:T(8,128)}, u32[]{:S(2)}) copy-start(f32[2,32,256]{2,1,0:T(8,128)} %constant.10.clone.core_hbm) | copy-start | bytes 196612
  0.0 11.0 %copy-start.3 = (f32[3,3072]{1,0:T(4,128)S(1)}, f32[3,3072]{1,0:T(4,128)}, u32[]{:S(2)}) copy-start(f32[3,3072]{1,0:T(4,128)} %taps_ref.1) | copy-start | bytes 110596
  0.0 11.0 %copy-start.5 = (f32[64]{0:T(128)S(1)}, f32[64]{0:T(128)}, u32[]{:S(2)}) copy-start(f32[64]{0:T(128)} %param.15) | copy-start | bytes 772
  0.0 11.0 %copy-start.4 = (f32[64,2048]{1,0:T(8,128)S(1)}, f32[64,2048]{1,0:T(8,128)}, u32[]{:S(2)}) copy-start(f32[64,2048]{1,0:T(8,128)} %kernel_hbm.1) | copy-start | bytes 1572868
  0.0 17.1 %copy-start.6 = (bf16[2,256,256]{2,1,0:T(8,128)(2,1)S(1)}, bf16[2,256,256]{2,1,0:T(8,128)(2,1)}, u32[]{:S(2)}) copy-start(bf16[2,256,256]{2,1,0:T(8,128)(2,1)} %constant.11.clone.mix_hbm) | copy-start | bytes 786436
  3.4 10.0 %copy-start.10 = (f32[8,256]{1,0:T(8,128)S(1)}, f32[8,256]{1,0:T(8,128)}, u32[]{:S(2)}) copy-start(f32[8,256]{1,0:T(8,128)} %get-tuple-element.38) | copy-start | bytes 24580
  3.4 12.3 %copy-start.9 = (f32[8,256]{1,0:T(8,128)S(1)}, f32[8,256]{1,0:T(8,128)}, u32[]{:S(2)}) copy-start(f32[8,256]{1,0:T(8,128)} %get-tuple-element.39) | copy-start | bytes 24580
  3.4 22.6 %all-to-all-start = ((bf16[16,136,128]{2,1,0:T(8,128)(2,1)}), bf16[16,136,128]{2,1,0:T(8,128)(2,1)S(1)}, u32[]{:S(2)}, u32[]{:S(2)}) async-start(bf16[16,136,128]{2,1,0:T(8,128)(2,1)} %get-tuple-element.32), calls=%async_computation | async-start | bytes 1114112 | tf_op jit(solution)/shard_map/all_to_all | solution.py:636
  13.5 4.6 %collective-permute-start = (f32[8,256]{1,0:T(8,128)S(1)}, f32[8,256]{1,0:T(8,128)S(1)}, u32[]{:S(2)}, u32[]{:S(2)}) collective-permute-start(f32[8,256]{1,0:T(8,128)S(1)} %copy-done.10), channel_id=1, source_target_pairs={{0,1},{1,2},{2,3},{3,4},{4,5},{5,6},{6,7},{7,8},{8,9},{9,10},{10,1... | collective-permute-start | bytes 24584 | tf_op jit(solution)/shard_map/ppermute | solution.py:642
  15.8 4.2 %collective-permute-start.1 = (f32[8,256]{1,0:T(8,128)S(1)}, f32[8,256]{1,0:T(8,128)S(1)}, u32[]{:S(2)}, u32[]{:S(2)}) collective-permute-start(f32[8,256]{1,0:T(8,128)S(1)} %copy-done.9), channel_id=1, source_target_pairs={{1,0},{2,1},{3,2},{4,3},{5,4},{6,5},{7,6},{8,7},{9,8},{10,9},{11,1... | collective-permute-start | bytes 24584 | tf_op jit(solution)/shard_map/ppermute | solution.py:642
  26.0 20.9 %copy-start = (bf16[128,3072]{1,0:T(8,128)(2,1)S(1)}, bf16[128,3072]{1,0:T(8,128)(2,1)}, u32[]{:S(2)}) copy-start(bf16[128,3072]{1,0:T(8,128)(2,1)} %fwd_ref.1) | copy-start | bytes 2359300
  26.0 20.9 %copy-start.1 = (bf16[128,3072]{1,0:T(8,128)(2,1)S(1)}, bf16[128,3072]{1,0:T(8,128)(2,1)}, u32[]{:S(2)}) copy-start(bf16[128,3072]{1,0:T(8,128)(2,1)} %rev_ref.1) | copy-start | bytes 2359300
  26.0 20.9 %copy-start.2 = (bf16[1024,1024]{1,0:T(8,128)(2,1)S(1)}, bf16[1024,1024]{1,0:T(8,128)(2,1)}, u32[]{:S(2)}) copy-start(bf16[1024,1024]{1,0:T(8,128)(2,1)} %weight_ref.1) | copy-start | bytes 6291460

commit v3 on v2

--- a/solution.py
+++ b/solution.py
@@ -16,7 +16,7 @@
 EXTRA = 8
 LANES = 128
 TILE = 16
-CHUNK = 32
+CHUNK = 64
 BIN_GROUP = 2
 VMEM_BYTES = 30 * 1024 * 1024
 EDGE_LANES = 256
@@ -77,6 +77,12 @@
     if lanes == LANES:
         return pltpu.roll(value, lanes // 2, 1)
     return jnp.concatenate([value[:, lanes // 2 :], value[:, : lanes // 2]], axis=1)
+
+
+def trade(one, two):
+    left = lanes_of(one.shape) < one.shape[1] // 2
+    middle = swap(jnp.where(left, two, one))
+    return jnp.where(left, one, middle), jnp.where(left, middle, two)
 
 
 def left_halves(one, two):
@@ -249,6 +255,11 @@
         right = pltpu.roll(right, right_shift, 1) if right_shift else right
         return jnp.where(lanes_of(left.shape) < count, left, right)[:, :lanes].astype(jnp.bfloat16)
 
+    def pieces_of(left, right):
+        if pieces != 2:
+            return [piece_of(left, right, piece) for piece in range(pieces)]
+        return [value.astype(jnp.bfloat16) for value in trade(left, right)]
+
     def rows_of(ref, columns, start):
         return ref[start : start + TILE, columns].astype(jnp.float32)
 
@@ -299,10 +310,8 @@
                 edge = with_rows(edge, 4, rows_of(rev_ref, at_q, 0)[:EXTRA], 0)
                 rev_body = jnp.concatenate([rev_body, edge], axis=0)
                 rev_o_ref[place] = raw_o[:EDGE_ROWS]
-            for piece in range(pieces):
-                out_ref[block * pieces + piece, start : start + fwd_body.shape[0], :] = piece_of(
-                    fwd_body, rev_body, piece
-                )
+            for piece, value in enumerate(pieces_of(fwd_body, rev_body)):
+                out_ref[block * pieces + piece, start : start + value.shape[0], :] = value
         part = (slice(None), pl.ds(start, CHUNK + (EXTRA if final else 0)))
         copy = pltpu.make_async_copy(out_ref.at[part], out_hbm.at[part], out_sems.at[step])
         copy.start()
@@ -561,7 +570,8 @@
 
 
 def mixing_kernel(
-    ret_ref, fwd_o_ref, rev_o_ref, fwd_ref, rev_ref, taps_ref, weight_ref, out_ref, combined, total
+    ret_ref, fwd_o_ref, rev_o_ref, fwd_ref, rev_ref, taps_ref, weight_ref, out_hbm,
+    combined, total, out_ref, sems
 ):
     rows = fwd_ref.shape[0]
     width = weight_ref.shape[0]
@@ -580,43 +590,61 @@
         shift = (target - at_row + start) % EXTRA
         return pltpu.roll(tile, shift, 0) if shift else tile
 
-    def columns(block, which):
-        chunks = [
-            ret_ref[block * pieces + piece].astype(jnp.float32)[
-                :, which * count : (which + 1) * count
-            ]
-            for piece in range(pieces)
+    def columns(block):
+        chunks = [ret_ref[block * pieces + piece].astype(jnp.float32) for piece in range(pieces)]
+        if pieces == 2:
+            return trade(*chunks)
+        return [
+            jnp.concatenate([c[:, which * count : (which + 1) * count] for c in chunks], axis=1)
+            for which in range(2)
         ]
-        return jnp.concatenate(chunks, axis=1)
-
-    for block in range(blocks):
+
+    def fwd_gate(block):
         low = 2 * width + block * LANES
         taps = taps_ref[:, low : low + LANES]
         mixed = short_filter(fwd_ref[:, low : low + LANES].astype(jnp.float32), taps, False)
         more = jnp.where(edge_row < 2, taps[2:3] * near_edge(fwd_o_ref, block, 0), 0.0)
         last = jnp.where(edge_row == 0, taps[1:2] * near_edge(fwd_o_ref, block, -1), 0.0)
-        mixed = jnp.concatenate([mixed[:EXTRA] + more + last, mixed[EXTRA:]], axis=0)
-        gated = mixed * columns(block, 0)
-
-        other = blocks - 1 - block
-        low = 2 * width + other * LANES
+        return jnp.concatenate([mixed[:EXTRA] + more + last, mixed[EXTRA:]], axis=0)
+
+    def rev_gate(block):
+        low = 2 * width + block * LANES
         taps = taps_ref[:, low : low + LANES]
         mixed = short_filter(rev_ref[:, low : low + LANES].astype(jnp.float32), taps, True)
-        more = jnp.where(edge_row >= 6, taps[2:3] * near_edge(rev_o_ref, other, 6), 0.0)
-        first = jnp.where(edge_row == 7, taps[1:2] * near_edge(rev_o_ref, other, 7), 0.0)
+        more = jnp.where(edge_row >= 6, taps[2:3] * near_edge(rev_o_ref, block, 6), 0.0)
+        first = jnp.where(edge_row == 7, taps[1:2] * near_edge(rev_o_ref, block, 7), 0.0)
         tail = mixed[rows - EXTRA :] + more + first
-        mixed = jnp.concatenate([mixed[: rows - EXTRA], tail], axis=0)
-        turned = jnp.take_along_axis(mixed * columns(other, 1), mirror, axis=1)
-        combined[:, block * LANES : (block + 1) * LANES] = (gated + turned).astype(jnp.bfloat16)
-        if block % 2:
-            part = slice((block - 1) * LANES, (block + 1) * LANES)
-            product = dot(combined[:, part], weight_ref[part, :])
-            if block == 1:
-                total[...] = product
-            elif block < blocks - 1:
-                total[...] += product
-            else:
-                out_ref[...] = (total[...] + product).astype(jnp.bfloat16)
+        return jnp.concatenate([mixed[: rows - EXTRA], tail], axis=0)
+
+    def product_of(start, end):
+        part = slice(start * LANES, end * LANES)
+        return dot(combined[:, part], weight_ref[part, :])
+
+    half = blocks // 2
+    for block in range(half):
+        pair = (block, blocks - 1 - block)
+        found = [columns(b) for b in pair]
+        for at, b in enumerate(pair):
+            gated = fwd_gate(b) * found[at][0]
+            gate = rev_gate(pair[1 - at]) * found[1 - at][1]
+            turned = jnp.take_along_axis(gate, mirror, axis=1)
+            combined[:, b * LANES : (b + 1) * LANES] = (gated + turned).astype(jnp.bfloat16)
+        if 2 * block + 2 == half:
+            total[...] = product_of(0, block + 1) + product_of(blocks - 1 - block, blocks)
+    middle = half // 2
+    part = slice(middle * LANES, (blocks - middle) * LANES)
+    copies = []
+    for side in range(2):
+        columns_out = pl.ds(side * (width // 2), width // 2)
+        product = dot(combined[:, part], weight_ref[part, columns_out])
+        out_ref[:, columns_out] = (total[:, columns_out] + product).astype(jnp.bfloat16)
+        copy = pltpu.make_async_copy(
+            out_ref.at[:, columns_out], out_hbm.at[:, columns_out], sems.at[side]
+        )
+        copy.start()
+        copies.append(copy)
+    for copy in copies:
+        copy.wait()
 
 
 HBM = pl.BlockSpec(memory_space=pltpu.HBM)
@@ -763,10 +791,12 @@
         mixing_kernel,
         out_shape=jax.ShapeDtypeStruct((rows, width), jnp.bfloat16),
         in_specs=[VMEM] * 7,
-        out_specs=VMEM,
+        out_specs=HBM,
         scratch_shapes=[
             pltpu.VMEM((rows, width), jnp.bfloat16),
             pltpu.VMEM((rows, width), jnp.float32),
+            pltpu.VMEM((rows, width), jnp.bfloat16),
+            pltpu.SemaphoreType.DMA((2,)),
         ],
         compiler_params=params(),
         cost_estimate=cost(2 * rows * width * width, 4 * 1024 * 1024),

time: 48.9 us -> 48.6 us (level)
  no operation moved by 1% of the time
where the time goes in v3:
time: 48.6 us; the launch traced here: 48.2 us
  blocking collectives  18.5 us (38%)
  starting transfers between devices  11.1 us (23%)
  Pallas kernels  10.4 us (21%)
  waiting for transfers between devices  7.93 us (16%)
    all_to_all x1, blocking collectives, exchange(): return lax.all_to_all(value, 'ctx', split_axis=0, concat_axis=0, tiled=True)  18.5 us
    all_to_all x1, starting transfers between devices, exchange(): return lax.all_to_all(value, 'ctx', split_axis=0, concat_axis=0, tiled=True)  7.54 us
    all_to_all x1, waiting for transfers between devices, exchange(): return lax.all_to_all(value, 'ctx', split_axis=0, concat_axis=0, tiled=True)  6.03 us
    ppermute x2, starting transfers between devices, shifted(): lax.ppermute(value, 'ctx', [(source, source + steps) for source in range(...  3.6 us
    pallas_call x1, Pallas kernels, per_device(): pl.pallas_call(gate_kernel, out_shape=(jax.ShapeDtypeStruct(block, jnp.bf...  3.12 us
    pallas_call x1, Pallas kernels, per_device(): pl.pallas_call(sections_kernel, out_shape=(section_shape, section_shape,...  2.39 us
    pallas_call x1, Pallas kernels, per_device(): pl.pallas_call(filter_kernel, out_shape=jax.ShapeDtypeStruct((HALF, per,...  2.33 us
    ppermute x2, waiting for transfers between devices, shifted(): lax.ppermute(value, 'ctx', [(source, source + steps) for source in range(...  1.9 us
  transfers between devices with their start and end apart: 3, of which 2 were waited for; matrix products, arithmetic and copies ran while one was open for 0% of the time, Pallas kernels for 7%

profile of v3, /device:TPU:0, one launch (start us, length us, event | category | flops | bytes accessed | tf_op | source)
XLA Modules:
  0.0 48.2 jit_solution(4017954957405521270)
XLA Ops:
  0.0 0.0 copy-start.7
  0.0 0.0 copy-start.8
  0.0 0.0 copy-start.3
  0.0 0.0 copy-start.5
  0.0 0.0 copy-start.4
  0.0 0.0 copy-start.6
  0.0 3.1 %gate.1 = (bf16[16,136,128]{2,1,0:T(8,128)(2,1)}, f32[8,256]{1,0:T(8,128)}, f32[8,256]{1,0:T(8,128)}) custom-call(bf16[128,3072]{1,0:T(8,128)(2,1)} %fwd_ref.1, bf16[128,3072]{1,0:T(8,128)(2,1)} %rev_ref.1, s32[1,128]{1,0:T(1,128)} %bitcast.8, f32[3,3072]{1,0:T(4,128)} %taps_ref.1), custom_call_target="tpu_custom_call" | custom-call | tf_op jit(solution)/shard_map/gate/pallas_call | solution.py:689
  3.2 0.0 copy-start.10
  3.2 0.0 copy-start.9
  3.2 7.5 %all-to-all-start = ((bf16[16,136,128]{2,1,0:T(8,128)(2,1)}), bf16[16,136,128]{2,1,0:T(8,128)(2,1)S(1)}, u32[]{:S(2)}, u32[]{:S(2)}) async-start(bf16[16,136,128]{2,1,0:T(8,128)(2,1)} %get-tuple-element.32), calls=%async_computation | async-start | bytes 1114112 | tf_op jit(solution)/shard_map/all_to_all | solution.py:664
  10.7 0.0 copy-done.7
  10.7 0.0 copy-done.8
  10.8 0.0 copy-done.3
  10.8 0.0 copy-done.5
  10.8 0.0 copy-done.4
  10.8 2.4 %sections.1 = (bf16[9,256,128]{2,1,0:T(8,128)(2,1)S(1)}, bf16[9,256,128]{2,1,0:T(8,128)(2,1)S(1)}, f32[8,128]{1,0:T(8,128)S(1)}, f32[32,256]{1,0:T(8,128)S(1)}, f32[128,128]{1,0:T(8,128)S(1)}) custom-call(s32[1]{0:T(128)} %bitcast.1.me_ref, f32[64,2048]{1,0:T(8,128)S(1)} %copy-done.4, f32[1,64]{1,0:T(1,128)S(1)} %bitcast.7, f32[3,3072]{1,0:T(4,128)S(1)} %copy-done.3, ...), custom_call_target="tpu_custom_call" | custom-call | flops 452984832 | bytes 4194304 | tf_op jit(solution)/shard_map/sections/pallas_call | solution.py:723
  13.2 0.0 copy-done.10
  13.2 2.3 %collective-permute-start = (f32[8,256]{1,0:T(8,128)S(1)}, f32[8,256]{1,0:T(8,128)S(1)}, u32[]{:S(2)}, u32[]{:S(2)}) collective-permute-start(f32[8,256]{1,0:T(8,128)S(1)} %copy-done.10), channel_id=1, source_target_pairs={{0,1},{1,2},{2,3},{3,4},{4,5},{5,6},{6,7},{7,8},{8,9},{9,10},{10,1... | collective-permute-start | bytes 24584 | tf_op jit(solution)/shard_map/ppermute | solution.py:670
  15.5 0.0 copy-done.9
  15.5 1.3 %collective-permute-start.1 = (f32[8,256]{1,0:T(8,128)S(1)}, f32[8,256]{1,0:T(8,128)S(1)}, u32[]{:S(2)}, u32[]{:S(2)}) collective-permute-start(f32[8,256]{1,0:T(8,128)S(1)} %copy-done.9), channel_id=1, source_target_pairs={{1,0},{2,1},{3,2},{4,3},{5,4},{6,5},{7,6},{8,7},{9,8},{10,9},{11,1... | collective-permute-start | bytes 24584 | tf_op jit(solution)/shard_map/ppermute | solution.py:670
  16.8 0.0 copy-done.6
  16.8 1.0 %spectrum.1 = (f32[2,256,128]{2,1,0:T(8,128)S(1)}, f32[2,256,128]{2,1,0:T(8,128)S(1)}, f32[2,256,128]{2,1,0:T(8,128)S(1)}, f32[2,256,128]{2,1,0:T(8,128)S(1)}, f...) custom-call(bf16[9,256,128]{2,1,0:T(8,128)(2,1)S(1)} %get-tuple-elem, ...), custom_call_target="tpu_custom_call" | custom-call | flops 452984832 | bytes 4194304 | tf_op jit(solution)/shard_map/spectrum/pallas_call | solution.py:755
  17.8 0.0 collective-permute-done.fwd_o_ref
  17.8 1.9 %collective-permute-done.1.rev_o_ref = f32[8,256]{1,0:T(8,128)S(1)} collective-permute-done((f32[8,256]{1,0:T(8,128)S(1)}, f32[8,256]{1,0:T(8,128)S(1)}, u32[]{:S(2)}, u32[]{:S(2)}) %collective-permute-start.1) | collective-permute-done | bytes 8224 | tf_op jit(solution)/shard_map/ppermute | solution.py:670
  19.7 6.0 %all-to-all-done = bf16[16,136,128]{2,1,0:T(8,128)(2,1)S(1)} async-done(((bf16[16,136,128]{2,1,0:T(8,128)(2,1)}), bf16[16,136,128]{2,1,0:T(8,128)(2,1)S(1)}, u32[]{:S(2)}, u32[]{:S(2)}) %all-to-all-start) | async-done | bytes 557088 | tf_op jit(solution)/shard_map/all_to_all | solution.py:664
  25.8 0.0 copy-start
  25.8 0.0 copy-start.1
  25.8 0.0 copy-start.2
  25.8 2.3 %filter.1 = bf16[16,1,128,128]{3,2,1,0:T(8,128)(2,1)S(1)} custom-call(bf16[16,1,136,128]{3,2,1,0:T(8,128)(2,1)S(1)} %bitcast.5, f32[8,128]{1,0:T(8,128)S(1)} %get-tuple-element.40.own_taps_ref, f32[32,256]{1,0:T(8,128)S(1)} %get-tuple-element.41.core_ref, f32[128,128]{1,0:T(8,128)S(1)} %get-tuple-element.42.turn_ref, ...), custom_call_target="tpu_custom_call" | custom-call | flops 1207959552 | bytes 4194304 | tf_op jit(solution)/shard_map/filter/pallas_call | solution.py:772
  28.1 18.5 %all_to_all.10.ret_ref = bf16[16,128,128]{2,1,0:T(8,128)(2,1)S(1)} all-to-all(bf16[16,128,128]{2,1,0:T(8,128)(2,1)S(1)} %bitcast.6), channel_id=1, replica_groups=mesh['dp'=2,'ctx'=16] {'ctx'}, dimensions={0} | all-to-all | bytes 1048576 | tf_op jit(solution)/shard_map/all_to_all | solution.py:664
  46.6 0.0 copy-done
  46.6 0.0 copy-done.1
  46.6 0.0 copy-done.2
  46.6 1.6 %mixing.1 = bf16[128,1024]{1,0:T(8,128)(2,1)} custom-call(bf16[16,128,128]{2,1,0:T(8,128)(2,1)S(1)} %all_to_all.10.ret_ref, f32[8,256]{1,0:T(8,128)S(1)} %collective-permute-done.fwd_o_ref, f32[8,256]{1,0:T(8,128)S(1)} %collective-permute-done.1.rev_o_ref, bf16[128,3072]{1,0:T(8,128)(2,1)S(1)} %copy-done, bf16[128,3072]{1,0:T(8,128)(2,1)S(1)} %copy-done.1, ...), custom_call_target="tpu_custom_call" | custom-call | flops 268435456 | bytes 4194304 | tf_op jit(solution)/shard_map/mixing/pallas_call | solution.py:790
Async XLA Ops:
  0.0 10.7 %copy-start.7 = (f32[128,128]{1,0:T(8,128)S(1)}, f32[128,128]{1,0:T(8,128)}, u32[]{:S(2)}) copy-start(f32[128,128]{1,0:T(8,128)} %constant.12.clone.phase_hbm) | copy-start | bytes 196612
  0.0 10.7 %copy-start.8 = (f32[2,32,256]{2,1,0:T(8,128)S(1)}, f32[2,32,256]{2,1,0:T(8,128)}, u32[]{:S(2)}) copy-start(f32[2,32,256]{2,1,0:T(8,128)} %constant.10.clone.core_hbm) | copy-start | bytes 196612
  0.0 10.8 %copy-start.3 = (f32[3,3072]{1,0:T(4,128)S(1)}, f32[3,3072]{1,0:T(4,128)}, u32[]{:S(2)}) copy-start(f32[3,3072]{1,0:T(4,128)} %taps_ref.1) | copy-start | bytes 110596
  0.0 10.8 %copy-start.5 = (f32[64]{0:T(128)S(1)}, f32[64]{0:T(128)}, u32[]{:S(2)}) copy-start(f32[64]{0:T(128)} %param.15) | copy-start | bytes 772
  0.0 10.8 %copy-start.4 = (f32[64,2048]{1,0:T(8,128)S(1)}, f32[64,2048]{1,0:T(8,128)}, u32[]{:S(2)}) copy-start(f32[64,2048]{1,0:T(8,128)} %kernel_hbm.1) | copy-start | bytes 1572868
  0.0 16.8 %copy-start.6 = (bf16[2,256,256]{2,1,0:T(8,128)(2,1)S(1)}, bf16[2,256,256]{2,1,0:T(8,128)(2,1)}, u32[]{:S(2)}) copy-start(bf16[2,256,256]{2,1,0:T(8,128)(2,1)} %constant.11.clone.mix_hbm) | copy-start | bytes 786436
  3.2 10.0 %copy-start.10 = (f32[8,256]{1,0:T(8,128)S(1)}, f32[8,256]{1,0:T(8,128)}, u32[]{:S(2)}) copy-start(f32[8,256]{1,0:T(8,128)} %get-tuple-element.38) | copy-start | bytes 24580
  3.2 12.3 %copy-start.9 = (f32[8,256]{1,0:T(8,128)S(1)}, f32[8,256]{1,0:T(8,128)}, u32[]{:S(2)}) copy-start(f32[8,256]{1,0:T(8,128)} %get-tuple-element.39) | copy-start | bytes 24580
  3.2 22.6 %all-to-all-start = ((bf16[16,136,128]{2,1,0:T(8,128)(2,1)}), bf16[16,136,128]{2,1,0:T(8,128)(2,1)S(1)}, u32[]{:S(2)}, u32[]{:S(2)}) async-start(bf16[16,136,128]{2,1,0:T(8,128)(2,1)} %get-tuple-element.32), calls=%async_computation | async-start | bytes 1114112 | tf_op jit(solution)/shard_map/all_to_all | solution.py:664
  13.2 4.6 %collective-permute-start = (f32[8,256]{1,0:T(8,128)S(1)}, f32[8,256]{1,0:T(8,128)S(1)}, u32[]{:S(2)}, u32[]{:S(2)}) collective-permute-start(f32[8,256]{1,0:T(8,128)S(1)} %copy-done.10), channel_id=1, source_target_pairs={{0,1},{1,2},{2,3},{3,4},{4,5},{5,6},{6,7},{7,8},{8,9},{9,10},{10,1... | collective-permute-start | bytes 24584 | tf_op jit(solution)/shard_map/ppermute | solution.py:670
  15.5 4.2 %collective-permute-start.1 = (f32[8,256]{1,0:T(8,128)S(1)}, f32[8,256]{1,0:T(8,128)S(1)}, u32[]{:S(2)}, u32[]{:S(2)}) collective-permute-start(f32[8,256]{1,0:T(8,128)S(1)} %copy-done.9), channel_id=1, source_target_pairs={{1,0},{2,1},{3,2},{4,3},{5,4},{6,5},{7,6},{8,7},{9,8},{10,9},{11,1... | collective-permute-start | bytes 24584 | tf_op jit(solution)/shard_map/ppermute | solution.py:670
  25.8 20.9 %copy-start = (bf16[128,3072]{1,0:T(8,128)(2,1)S(1)}, bf16[128,3072]{1,0:T(8,128)(2,1)}, u32[]{:S(2)}) copy-start(bf16[128,3072]{1,0:T(8,128)(2,1)} %fwd_ref.1) | copy-start | bytes 2359300
  25.8 20.9 %copy-start.1 = (bf16[128,3072]{1,0:T(8,128)(2,1)S(1)}, bf16[128,3072]{1,0:T(8,128)(2,1)}, u32[]{:S(2)}) copy-start(bf16[128,3072]{1,0:T(8,128)(2,1)} %rev_ref.1) | copy-start | bytes 2359300
  25.8 20.9 %copy-start.2 = (bf16[1024,1024]{1,0:T(8,128)(2,1)S(1)}, bf16[1024,1024]{1,0:T(8,128)(2,1)}, u32[]{:S(2)}) copy-start(bf16[1024,1024]{1,0:T(8,128)(2,1)} %weight_ref.1) | copy-start | bytes 6291460

commit v4 on v3

--- a/solution.py
+++ b/solution.py
@@ -312,10 +312,17 @@
                 rev_o_ref[place] = raw_o[:EDGE_ROWS]
             for piece, value in enumerate(pieces_of(fwd_body, rev_body)):
                 out_ref[block * pieces + piece, start : start + value.shape[0], :] = value
-        part = (slice(None), pl.ds(start, CHUNK + (EXTRA if final else 0)))
-        copy = pltpu.make_async_copy(out_ref.at[part], out_hbm.at[part], out_sems.at[step])
-        copy.start()
-        stores.append(copy)
+            wide = width // LANES // 2
+            if block % wide == wide - 1:
+                part = (
+                    pl.ds((block + 1 - wide) * pieces, wide * pieces),
+                    pl.ds(start, CHUNK + (EXTRA if final else 0)),
+                )
+                copy = pltpu.make_async_copy(
+                    out_ref.at[part], out_hbm.at[part], out_sems.at[step, block // wide]
+                )
+                copy.start()
+                stores.append(copy)
     for at, (source, target) in enumerate(((fwd_o_ref, fwd_o_hbm), (rev_o_ref, rev_o_hbm))):
         copy = pltpu.make_async_copy(source, target, small_sems.at[4 + at])
         copy.start()
@@ -708,7 +715,7 @@
             pltpu.VMEM((EXTRA, width), jnp.float32),
             pltpu.SemaphoreType.DMA((rows // CHUNK, 2)),
             pltpu.SemaphoreType.DMA((6,)),
-            pltpu.SemaphoreType.DMA((rows // CHUNK,)),
+            pltpu.SemaphoreType.DMA((rows // CHUNK, 2)),
         ],
         compiler_params=params(FULL_VMEM_BYTES),
         name="gate",

time: 48.6 us -> 48.5 us (level)
  no operation moved by 1% of the time
where the time goes in v4:
time: 48.5 us; the launch traced here: 48.2 us
  blocking collectives  18.5 us (38%)
  starting transfers between devices  11.1 us (23%)
  Pallas kernels  10.4 us (21%)
  waiting for transfers between devices  7.93 us (16%)
    all_to_all x1, blocking collectives, exchange(): return lax.all_to_all(value, 'ctx', split_axis=0, concat_axis=0, tiled=True)  18.5 us
    all_to_all x1, starting transfers between devices, exchange(): return lax.all_to_all(value, 'ctx', split_axis=0, concat_axis=0, tiled=True)  7.54 us
    all_to_all x1, waiting for transfers between devices, exchange(): return lax.all_to_all(value, 'ctx', split_axis=0, concat_axis=0, tiled=True)  6.03 us
    ppermute x2, starting transfers between devices, shifted(): lax.ppermute(value, 'ctx', [(source, source + steps) for source in range(...  3.6 us
    pallas_call x1, Pallas kernels, per_device(): pl.pallas_call(gate_kernel, out_shape=(jax.ShapeDtypeStruct(block, jnp.bf...  3.07 us
    pallas_call x1, Pallas kernels, per_device(): pl.pallas_call(sections_kernel, out_shape=(section_shape, section_shape,...  2.39 us
    pallas_call x1, Pallas kernels, per_device(): pl.pallas_call(filter_kernel, out_shape=jax.ShapeDtypeStruct((HALF, per,...  2.33 us
    ppermute x2, waiting for transfers between devices, shifted(): lax.ppermute(value, 'ctx', [(source, source + steps) for source in range(...  1.9 us
  transfers between devices with their start and end apart: 3, of which 2 were waited for; matrix products, arithmetic and copies ran while one was open for 0% of the time, Pallas kernels for 7%

profile of v4, /device:TPU:0, one launch (start us, length us, event | category | flops | bytes accessed | tf_op | source)
XLA Modules:
  0.0 48.2 jit_solution(11930846150296294747)
XLA Ops:
  0.0 0.0 copy-start.7
  0.0 0.0 copy-start.8
  0.0 0.0 copy-start.3
  0.0 0.0 copy-start.5
  0.0 0.0 copy-start.4
  0.0 0.0 copy-start.6
  0.0 3.1 %gate.1 = (bf16[16,136,128]{2,1,0:T(8,128)(2,1)}, f32[8,256]{1,0:T(8,128)}, f32[8,256]{1,0:T(8,128)}) custom-call(bf16[128,3072]{1,0:T(8,128)(2,1)} %fwd_ref.1, bf16[128,3072]{1,0:T(8,128)(2,1)} %rev_ref.1, s32[1,128]{1,0:T(1,128)} %bitcast.8, f32[3,3072]{1,0:T(4,128)} %taps_ref.1), custom_call_target="tpu_custom_call" | custom-call | tf_op jit(solution)/shard_map/gate/pallas_call | solution.py:696
  3.1 0.0 copy-start.10
  3.1 0.0 copy-start.9
  3.1 7.5 %all-to-all-start = ((bf16[16,136,128]{2,1,0:T(8,128)(2,1)}), bf16[16,136,128]{2,1,0:T(8,128)(2,1)S(1)}, u32[]{:S(2)}, u32[]{:S(2)}) async-start(bf16[16,136,128]{2,1,0:T(8,128)(2,1)} %get-tuple-element.32), calls=%async_computation | async-start | bytes 1114112 | tf_op jit(solution)/shard_map/all_to_all | solution.py:671
  10.7 0.0 copy-done.7
  10.7 0.0 copy-done.8
  10.7 0.0 copy-done.3
  10.7 0.0 copy-done.5
  10.7 0.0 copy-done.4
  10.7 2.4 %sections.1 = (bf16[9,256,128]{2,1,0:T(8,128)(2,1)S(1)}, bf16[9,256,128]{2,1,0:T(8,128)(2,1)S(1)}, f32[8,128]{1,0:T(8,128)S(1)}, f32[32,256]{1,0:T(8,128)S(1)}, f32[128,128]{1,0:T(8,128)S(1)}) custom-call(s32[1]{0:T(128)} %bitcast.1.me_ref, f32[64,2048]{1,0:T(8,128)S(1)} %copy-done.4, f32[1,64]{1,0:T(1,128)S(1)} %bitcast.7, f32[3,3072]{1,0:T(4,128)S(1)} %copy-done.3, ...), custom_call_target="tpu_custom_call" | custom-call | flops 452984832 | bytes 4194304 | tf_op jit(solution)/shard_map/sections/pallas_call | solution.py:730
  13.1 0.0 copy-done.10
  13.1 2.3 %collective-permute-start = (f32[8,256]{1,0:T(8,128)S(1)}, f32[8,256]{1,0:T(8,128)S(1)}, u32[]{:S(2)}, u32[]{:S(2)}) collective-permute-start(f32[8,256]{1,0:T(8,128)S(1)} %copy-done.10), channel_id=1, source_target_pairs={{0,1},{1,2},{2,3},{3,4},{4,5},{5,6},{6,7},{7,8},{8,9},{9,10},{10,1... | collective-permute-start | bytes 24584 | tf_op jit(solution)/shard_map/ppermute | solution.py:677
  15.5 0.0 copy-done.9
  15.5 1.3 %collective-permute-start.1 = (f32[8,256]{1,0:T(8,128)S(1)}, f32[8,256]{1,0:T(8,128)S(1)}, u32[]{:S(2)}, u32[]{:S(2)}) collective-permute-start(f32[8,256]{1,0:T(8,128)S(1)} %copy-done.9), channel_id=1, source_target_pairs={{1,0},{2,1},{3,2},{4,3},{5,4},{6,5},{7,6},{8,7},{9,8},{10,9},{11,1... | collective-permute-start | bytes 24584 | tf_op jit(solution)/shard_map/ppermute | solution.py:677
  16.8 0.0 copy-done.6
  16.8 1.0 %spectrum.1 = (f32[2,256,128]{2,1,0:T(8,128)S(1)}, f32[2,256,128]{2,1,0:T(8,128)S(1)}, f32[2,256,128]{2,1,0:T(8,128)S(1)}, f32[2,256,128]{2,1,0:T(8,128)S(1)}, f...) custom-call(bf16[9,256,128]{2,1,0:T(8,128)(2,1)S(1)} %get-tuple-elem, ...), custom_call_target="tpu_custom_call" | custom-call | flops 452984832 | bytes 4194304 | tf_op jit(solution)/shard_map/spectrum/pallas_call | solution.py:762
  17.8 0.0 collective-permute-done.fwd_o_ref
  17.8 1.9 %collective-permute-done.1.rev_o_ref = f32[8,256]{1,0:T(8,128)S(1)} collective-permute-done((f32[8,256]{1,0:T(8,128)S(1)}, f32[8,256]{1,0:T(8,128)S(1)}, u32[]{:S(2)}, u32[]{:S(2)}) %collective-permute-start.1) | collective-permute-done | bytes 8224 | tf_op jit(solution)/shard_map/ppermute | solution.py:677
  19.7 6.0 %all-to-all-done = bf16[16,136,128]{2,1,0:T(8,128)(2,1)S(1)} async-done(((bf16[16,136,128]{2,1,0:T(8,128)(2,1)}), bf16[16,136,128]{2,1,0:T(8,128)(2,1)S(1)}, u32[]{:S(2)}, u32[]{:S(2)}) %all-to-all-start) | async-done | bytes 557088 | tf_op jit(solution)/shard_map/all_to_all | solution.py:671
  25.7 0.0 copy-start
  25.7 0.0 copy-start.1
  25.7 0.0 copy-start.2
  25.7 2.3 %filter.1 = bf16[16,1,128,128]{3,2,1,0:T(8,128)(2,1)S(1)} custom-call(bf16[16,1,136,128]{3,2,1,0:T(8,128)(2,1)S(1)} %bitcast.5, f32[8,128]{1,0:T(8,128)S(1)} %get-tuple-element.40.own_taps_ref, f32[32,256]{1,0:T(8,128)S(1)} %get-tuple-element.41.core_ref, f32[128,128]{1,0:T(8,128)S(1)} %get-tuple-element.42.turn_ref, ...), custom_call_target="tpu_custom_call" | custom-call | flops 1207959552 | bytes 4194304 | tf_op jit(solution)/shard_map/filter/pallas_call | solution.py:779
  28.0 18.5 %all_to_all.10.ret_ref = bf16[16,128,128]{2,1,0:T(8,128)(2,1)S(1)} all-to-all(bf16[16,128,128]{2,1,0:T(8,128)(2,1)S(1)} %bitcast.6), channel_id=1, replica_groups=mesh['dp'=2,'ctx'=16] {'ctx'}, dimensions={0} | all-to-all | bytes 1048576 | tf_op jit(solution)/shard_map/all_to_all | solution.py:671
  46.6 0.0 copy-done
  46.6 0.0 copy-done.1
  46.6 0.0 copy-done.2
  46.6 1.6 %mixing.1 = bf16[128,1024]{1,0:T(8,128)(2,1)} custom-call(bf16[16,128,128]{2,1,0:T(8,128)(2,1)S(1)} %all_to_all.10.ret_ref, f32[8,256]{1,0:T(8,128)S(1)} %collective-permute-done.fwd_o_ref, f32[8,256]{1,0:T(8,128)S(1)} %collective-permute-done.1.rev_o_ref, bf16[128,3072]{1,0:T(8,128)(2,1)S(1)} %copy-done, bf16[128,3072]{1,0:T(8,128)(2,1)S(1)} %copy-done.1, ...), custom_call_target="tpu_custom_call" | custom-call | flops 268435456 | bytes 4194304 | tf_op jit(solution)/shard_map/mixing/pallas_call | solution.py:797
Async XLA Ops:
  0.0 10.7 %copy-start.7 = (f32[128,128]{1,0:T(8,128)S(1)}, f32[128,128]{1,0:T(8,128)}, u32[]{:S(2)}) copy-start(f32[128,128]{1,0:T(8,128)} %constant.12.clone.phase_hbm) | copy-start | bytes 196612
  0.0 10.7 %copy-start.8 = (f32[2,32,256]{2,1,0:T(8,128)S(1)}, f32[2,32,256]{2,1,0:T(8,128)}, u32[]{:S(2)}) copy-start(f32[2,32,256]{2,1,0:T(8,128)} %constant.10.clone.core_hbm) | copy-start | bytes 196612
  0.0 10.7 %copy-start.3 = (f32[3,3072]{1,0:T(4,128)S(1)}, f32[3,3072]{1,0:T(4,128)}, u32[]{:S(2)}) copy-start(f32[3,3072]{1,0:T(4,128)} %taps_ref.1) | copy-start | bytes 110596
  0.0 10.7 %copy-start.5 = (f32[64]{0:T(128)S(1)}, f32[64]{0:T(128)}, u32[]{:S(2)}) copy-start(f32[64]{0:T(128)} %param.15) | copy-start | bytes 772
  0.0 10.7 %copy-start.4 = (f32[64,2048]{1,0:T(8,128)S(1)}, f32[64,2048]{1,0:T(8,128)}, u32[]{:S(2)}) copy-start(f32[64,2048]{1,0:T(8,128)} %kernel_hbm.1) | copy-start | bytes 1572868
  0.0 16.8 %copy-start.6 = (bf16[2,256,256]{2,1,0:T(8,128)(2,1)S(1)}, bf16[2,256,256]{2,1,0:T(8,128)(2,1)}, u32[]{:S(2)}) copy-start(bf16[2,256,256]{2,1,0:T(8,128)(2,1)} %constant.11.clone.mix_hbm) | copy-start | bytes 786436
  3.1 10.0 %copy-start.10 = (f32[8,256]{1,0:T(8,128)S(1)}, f32[8,256]{1,0:T(8,128)}, u32[]{:S(2)}) copy-start(f32[8,256]{1,0:T(8,128)} %get-tuple-element.38) | copy-start | bytes 24580
  3.1 12.3 %copy-start.9 = (f32[8,256]{1,0:T(8,128)S(1)}, f32[8,256]{1,0:T(8,128)}, u32[]{:S(2)}) copy-start(f32[8,256]{1,0:T(8,128)} %get-tuple-element.39) | copy-start | bytes 24580
  3.1 22.6 %all-to-all-start = ((bf16[16,136,128]{2,1,0:T(8,128)(2,1)}), bf16[16,136,128]{2,1,0:T(8,128)(2,1)S(1)}, u32[]{:S(2)}, u32[]{:S(2)}) async-start(bf16[16,136,128]{2,1,0:T(8,128)(2,1)} %get-tuple-element.32), calls=%async_computation | async-start | bytes 1114112 | tf_op jit(solution)/shard_map/all_to_all | solution.py:671
  13.1 4.6 %collective-permute-start = (f32[8,256]{1,0:T(8,128)S(1)}, f32[8,256]{1,0:T(8,128)S(1)}, u32[]{:S(2)}, u32[]{:S(2)}) collective-permute-start(f32[8,256]{1,0:T(8,128)S(1)} %copy-done.10), channel_id=1, source_target_pairs={{0,1},{1,2},{2,3},{3,4},{4,5},{5,6},{6,7},{7,8},{8,9},{9,10},{10,1... | collective-permute-start | bytes 24584 | tf_op jit(solution)/shard_map/ppermute | solution.py:677
  15.5 4.2 %collective-permute-start.1 = (f32[8,256]{1,0:T(8,128)S(1)}, f32[8,256]{1,0:T(8,128)S(1)}, u32[]{:S(2)}, u32[]{:S(2)}) collective-permute-start(f32[8,256]{1,0:T(8,128)S(1)} %copy-done.9), channel_id=1, source_target_pairs={{1,0},{2,1},{3,2},{4,3},{5,4},{6,5},{7,6},{8,7},{9,8},{10,9},{11,1... | collective-permute-start | bytes 24584 | tf_op jit(solution)/shard_map/ppermute | solution.py:677
  25.7 20.9 %copy-start = (bf16[128,3072]{1,0:T(8,128)(2,1)S(1)}, bf16[128,3072]{1,0:T(8,128)(2,1)}, u32[]{:S(2)}) copy-start(bf16[128,3072]{1,0:T(8,128)(2,1)} %fwd_ref.1) | copy-start | bytes 2359300
  25.7 20.9 %copy-start.1 = (bf16[128,3072]{1,0:T(8,128)(2,1)S(1)}, bf16[128,3072]{1,0:T(8,128)(2,1)}, u32[]{:S(2)}) copy-start(bf16[128,3072]{1,0:T(8,128)(2,1)} %rev_ref.1) | copy-start | bytes 2359300
  25.7 20.9 %copy-start.2 = (bf16[1024,1024]{1,0:T(8,128)(2,1)S(1)}, bf16[1024,1024]{1,0:T(8,128)(2,1)}, u32[]{:S(2)}) copy-start(bf16[1024,1024]{1,0:T(8,128)(2,1)} %weight_ref.1) | copy-start | bytes 6291460
